TPU v7x, 512 devices: a whole 4x4x16 slice. The times are simulated.
512 devices in a mesh: seq: 128 (over z, y, core), dp: 4 (over x).
Axes of the slice: x: 4, y: 4, z: 16, core: 2. Of those that a mesh axis runs over, the one named last changes fastest.
Arguments:
- context: bfloat16 [4, 65536, 1024], P('dp', 'seq'), may hold values from -24 to 24
- block_valid: int32 [4, 512], P('dp', 'seq'), may hold values from 0 to 1, as said below
- key_weight: bfloat16 [1024, 128], replicated, may hold values from -0.1875 to 0.1875
- value_weight: bfloat16 [1024, 128], replicated, may hold values from -0.1875 to 0.1875
- latent_queries: bfloat16 [4, 256, 1024], P('dp', 'seq')
- out_grad: bfloat16 [4, 256, 1024], P('dp', 'seq'), may hold values from -6 to 6
Outputs:
- attended: bfloat16 [4, 256, 1024], P('dp', 'seq')
- query_grad: bfloat16 [4, 256, 1024], P('dp', 'seq')
- context_grad: bfloat16 [4, 65536, 1024], P('dp', 'seq')
- key_weight_grad: float32 [1024, 128], replicated
- value_weight_grad: float32 [1024, 128], replicated
Inputs may be any that keep to these rules, and one draw needn't show every extreme that they name: `block_valid`: block 0 of every context is 1.
All inputs are finite; a program needn't handle non-finite values.
Results may differ from a plain program's by a relative error of at most 0.013.
The roundings to bfloat16 on the way count: a program that leaves them out, or rounds other values in their place, can miss the bound.
Values may be sent and summed in bfloat16 or wider, within the bound.
A program may use at most 64 MiB of HBM per device.

v0:
```python
import math

import jax
import jax.numpy as jnp
from jax import lax
from jax.sharding import PartitionSpec as P

H = 16
KVH = 2
HD = 64
BLK = 128


masked_score = -1e30


def heads_first(matrix, groups):
    row_count = matrix.shape[0]
    return matrix.reshape(row_count, KVH, groups, HD).transpose(1, 2, 0, 3)


def heads_last(stacked):
    kv_heads, per_group, row_count, head_size = stacked.shape
    return stacked.transpose(2, 0, 1, 3).reshape(row_count, kv_heads * per_group * head_size)


def shards(context, block_valid, key_weight, value_weight, latent_queries, out_grad):
    score_scale = HD ** (-0.5)
    groups = H // KVH
    tokens = context[0]
    length = tokens.shape[0]
    own_rows = latent_queries.shape[1]
    key_rows = (
        jnp.dot(tokens, key_weight, preferred_element_type=jnp.float32)
        .astype(jnp.bfloat16)
        .reshape(length, KVH, HD)
    )
    value_rows = (
        jnp.dot(tokens, value_weight, preferred_element_type=jnp.float32)
        .astype(jnp.bfloat16)
        .reshape(length, KVH, HD)
    )
    block_flags = block_valid[0] > 0
    live_keys = jnp.repeat(block_flags, BLK)
    block_width = math.gcd(length, 256)
    block_count = length // block_width
    queries = lax.all_gather(latent_queries, "seq", axis=1, tiled=True)[0]
    latents = queries.shape[0]
    grouped = heads_first(queries, groups)

    def block_scores(offset):
        key_part = lax.dynamic_slice_in_dim(key_rows, offset, block_width, 0)
        live_part = lax.dynamic_slice_in_dim(live_keys, offset, block_width, 0)
        scores = (
            jnp.einsum("cgld,kcd->cglk", grouped, key_part, preferred_element_type=jnp.float32)
            * score_scale
        )
        return (jnp.where(live_part[None, None, None, :], scores, masked_score), live_part)

    def sweep_blocks(update, initial):

        def advance(block_index, carried):
            offset = block_index * block_width
            return update(carried, offset)

        return lax.fori_loop(0, block_count, advance, initial)

    def peak_update(peaks, offset):
        scores, live_part = block_scores(offset)
        return jnp.maximum(peaks, jnp.max(scores, axis=-1))

    local_peaks = sweep_blocks(
        peak_update, jnp.full((KVH, groups, latents), masked_score, jnp.float32)
    )
    peaks = lax.pmax(local_peaks, "seq")

    def sum_update(carried, offset):
        totals, weighted = carried
        scores, live_part = block_scores(offset)
        probabilities = jnp.where(
            live_part[None, None, None, :], jnp.exp(scores - peaks[..., None]), 0.0
        )
        value_part = lax.dynamic_slice_in_dim(value_rows, offset, block_width, 0)
        weighted = weighted + jnp.einsum(
            "cglk,kcd->cgld",
            probabilities.astype(jnp.bfloat16),
            value_part,
            preferred_element_type=jnp.float32,
        )
        return (totals + jnp.sum(probabilities, axis=-1), weighted)

    start_sums = (
        jnp.zeros((KVH, groups, latents), jnp.float32),
        jnp.zeros((KVH, groups, latents, HD), jnp.float32),
    )
    totals, weighted = sweep_blocks(sum_update, start_sums)
    first_row = lax.axis_index("seq") * own_rows
    own_sums = lax.psum_scatter(heads_last(weighted), "seq", scatter_dimension=0, tiled=True)
    totals = lax.psum(totals, "seq")
    own_totals = lax.dynamic_slice_in_dim(totals, first_row, own_rows, 2)
    attended = heads_last(
        (heads_first(own_sums, groups) / own_totals[..., None]).astype(jnp.bfloat16)
    )
    grad_rows, full_rows = (
        lax.all_gather(out_grad[0], "seq", axis=0, tiled=True),
        lax.all_gather(attended, "seq", axis=0, tiled=True),
    )
    grad_heads = heads_first(grad_rows, groups)
    full_heads = heads_first(full_rows, groups)
    row_delta = jnp.sum(grad_heads.astype(jnp.float32) * full_heads.astype(jnp.float32), axis=-1)

    def grad_update(carried, offset):
        query_acc, key_acc, value_acc = carried
        scores, live_part = block_scores(offset)
        probabilities = jnp.where(
            live_part[None, None, None, :],
            jnp.exp(scores - peaks[..., None]) / totals[..., None],
            0.0,
        )
        key_part = lax.dynamic_slice_in_dim(key_rows, offset, block_width, 0)
        value_part = lax.dynamic_slice_in_dim(value_rows, offset, block_width, 0)
        slopes = jnp.einsum(
            "cgld,kcd->cglk", grad_heads, value_part, preferred_element_type=jnp.float32
        )
        score_grads = (probabilities * (slopes - row_delta[..., None])).astype(jnp.bfloat16)
        query_acc = query_acc + jnp.einsum(
            "cglk,kcd->cgld", score_grads, key_part, preferred_element_type=jnp.float32
        )
        key_grad = (
            jnp.einsum("cglk,cgld->kcd", score_grads, grouped, preferred_element_type=jnp.float32)
            * score_scale
        ).astype(jnp.bfloat16)
        value_grad = jnp.einsum(
            "cglk,cgld->kcd",
            probabilities.astype(jnp.bfloat16),
            grad_heads,
            preferred_element_type=jnp.float32,
        ).astype(jnp.bfloat16)
        key_acc = lax.dynamic_update_slice_in_dim(key_acc, key_grad, offset, 0)
        value_acc = lax.dynamic_update_slice_in_dim(value_acc, value_grad, offset, 0)
        return (query_acc, key_acc, value_acc)

    start_grads = (
        jnp.zeros((KVH, groups, latents, HD), jnp.float32),
        jnp.zeros((length, KVH, HD), jnp.bfloat16),
        jnp.zeros((length, KVH, HD), jnp.bfloat16),
    )
    query_acc, key_acc, value_acc = sweep_blocks(grad_update, start_grads)
    query_grad = lax.psum_scatter(
        heads_last(query_acc * score_scale), "seq", scatter_dimension=0, tiled=True
    ).astype(jnp.bfloat16)
    key_flat = key_acc.reshape(length, KVH * HD)
    value_flat = value_acc.reshape(length, KVH * HD)
    context_grad = (
        jnp.dot(key_flat, key_weight.T, preferred_element_type=jnp.float32)
        + jnp.dot(value_flat, value_weight.T, preferred_element_type=jnp.float32)
    ).astype(jnp.bfloat16)
    contract_rows = (((0,), (0,)), ((), ()))
    weight_k = lax.dot_general(tokens, key_flat, contract_rows, preferred_element_type=jnp.float32)
    weight_v = lax.dot_general(
        tokens, value_flat, contract_rows, preferred_element_type=jnp.float32
    )
    weight_k, weight_v = lax.psum((weight_k, weight_v), ("seq", "dp"))
    return (attended[None], query_grad[None], context_grad[None], weight_k, weight_v)


def solution(mesh):
    in_specs = (
        P("dp", "seq", None),
        P("dp", "seq"),
        P(),
        P(),
        P("dp", "seq", None),
        P("dp", "seq", None),
    )
    out_specs = (P("dp", "seq", None), P("dp", "seq", None), P("dp", "seq", None), P(), P())
    return jax.shard_map(shards, mesh=mesh, in_specs=in_specs, out_specs=out_specs, check_vma=False)
```

profile of v0, /device:TPU:1, one launch (start us, length us, event | category | flops | bytes accessed | tf_op | source)
XLA Modules:
  0.0 2315.1 jit_solution(14783957717837437849)
XLA Ops:
  7.2 0.0 all-reduce.7.cloned.1.call-start
  7.3 0.7 compare_bitcast_fusion
  8.0 0.1 broadcast_bitcast_fusion
  8.1 0.7 copy.64
  8.8 1.4 convolution_convert_fusion.1
  10.2 1.4 convolution_convert_fusion
  11.6 109.1 %all_gather.9 = bf16[1,256,1024]{2,0,1:T(2,128)(2,1)S(1)} all-gather(bf16[1,2,1024]{2,0,1:T(2,128)(2,1)S(1)} %copy.64), channel_id=1, replica_groups=mesh['seq'=128,'dp'=4] {'seq'}, dimensions={1}, use_global_device_ids=true | all-gather | bytes 528384 | tf_op jit(solution)/shard_map/all_gather | solution.py:47
  120.7 0.9 copy.65
  121.7 1.8 while.48
  121.7 0.1 dynamic_slice.106
  121.8 0.8 select_reduce_fusion.2
  122.6 0.1 dynamic_slice.106
  122.7 0.8 select_reduce_fusion.2
  123.5 488.0 %pmax.7 = f32[2,8,256]{2,1,0:T(8,128)S(1)} all-reduce(f32[2,8,256]{2,1,0:T(8,128)S(1)} %get-tuple-element.440), channel_id=1, replica_groups=mesh['seq'=128,'dp'=4] {'seq'}, use_global_device_ids=true, to_apply=%region_3.4 | all-reduce | flops 4096 | bytes 32768 | tf_op jit(solution)/shard_map/pmax | solution.py:75
  611.4 5.5 while.49
  611.4 0.1 dynamic_slice.109
  611.5 1.4 bitcast_reduce_fusion.2
  612.9 1.3 fusion.107
  614.2 0.1 dynamic_slice.109
  614.3 1.4 bitcast_reduce_fusion.2
  615.7 1.2 fusion.107
  617.0 0.9 copy-done.5
  618.0 0.0 all-reduce.9.cloned.1.call-start
  618.1 113.1 %all-gather = bf16[1,256,1024]{2,0,1:T(2,128)(2,1)} all-gather(bf16[1,2,1024]{2,0,1:T(2,128)(2,1)S(1)} %copy.66), channel_id=2, replica_groups=mesh['seq'=128,'dp'=4] {'seq'}, dimensions={1}, use_global_device_ids=true | all-gather | bytes 528384 | tf_op jit(solution)/shard_map/all_gather | solution.py:105
  731.1 2.3 copy.67
  733.5 1.3 dynamic-slice
  735.4 487.7 %psum.21 = f32[2,8,256]{2,1,0:T(8,128)S(1)} all-reduce(f32[2,8,256]{2,1,0:T(8,128)S(1)} %get-tuple-element.442), channel_id=1, replica_groups=mesh['seq'=128,'dp'=4] {'seq'}, use_global_device_ids=true, to_apply=%region_8.9 | all-reduce | flops 4096 | bytes 32768 | tf_op jit(solution)/shard_map/psum | solution.py:99
  1223.1 0.1 dynamic-slice_bitcast_fusion
  1223.2 2.0 fusion.68
  1225.1 1.1 copy.70
  1226.2 91.1 %all-gather.1 = bf16[128,2,1024]{2,1,0:T(2,128)(2,1)} all-gather(bf16[1,2,1024]{2,1,0:T(2,128)(2,1)S(1)} %copy.70), channel_id=1, replica_groups=mesh['seq'=128,'dp'=4] {'seq'}, dimensions={0}, use_global_device_ids=true | all-gather | bytes 528384 | tf_op jit(solution)/shard_map/all_gather | solution.py:106
  1317.3 3.1 reshape.65
  1320.4 3.5 copy.69
  1323.9 1.4 fusion.63
  1325.3 0.7 broadcast.72
  1325.9 11.7 while.50
  1325.9 0.7 dynamic_slice.113
  1326.6 2.1 divide_select_fusion.2
  1328.7 0.8 fusion.120
  1329.5 0.8 multiply_convert_fusion.2
  1330.2 0.1 copy-done.1
  1330.4 0.8 fusion.119
  1331.1 0.6 fusion.118
  1331.7 0.1 copy-done.2
  1331.8 0.7 dynamic_slice.113
  1332.4 2.1 divide_select_fusion.2
  1334.5 0.8 fusion.120
  1335.3 0.8 multiply_convert_fusion.2
  1336.1 0.1 copy-done.1
  1336.2 0.8 fusion.119
  1337.0 0.6 fusion.118
  1337.5 0.1 copy-done.2
  1337.6 1.1 convolution_bitcast_fusion
  1338.7 2.0 convolution_bitcast_fusion.1
  1340.7 1.1 broadcast_multiply_fusion
  1341.8 494.7 %all-reduce.10 = bf16[256,1024]{0,1:T(8,128)(2,1)S(1)} all-reduce(f32[256,1024]{0,1:T(8,128)} %bitcast.201), channel_id=4, replica_groups=mesh['seq'=128,'dp'=4] {'seq'}, use_global_device_ids=true, to_apply=%region_12.13.clone | all-reduce | flops 262144 | bytes 1572864
  1836.5 0.0 all-reduce.9.cloned.1.call-update
  1836.5 0.1 fusion.69
  1836.7 0.7 copy.71
  1837.4 0.5 fusion.70
  1837.9 2.4 fusion.62
  1840.2 463.9 %all-reduce.9.cloned.1.call-done = (f32[1024,128]{0,1:T(8,128)}, f32[1024,128]{0,1:T(8,128)}) async-done(((f32[1024,128]{0,1:T(8,128)}, f32[1024,128]{0,1:T(8,128)}), (f32[1024,128]{0,1:T(8,128)}, f32[1024,128]{0,1:T(8,128)})) %all-reduce.9.cloned.1.call-update) | async-done | bytes 1048592 | tf_op jit(solution)/shard_map/psum | solution.py:163
  2304.2 2.0 copy.72
  2306.2 2.0 copy.73
  (35 shorter events, 0.1 us)
Async XLA Ops:
  7.2 1.6 copy-start
  7.2 1216.0 %all-reduce.7.cloned.1.call-start = ((), (), s32[]{:S(2)}) async-start(), calls=%async_computation | async-start | bytes 2097152
  121.7 489.8 %copy-start.4 = (f32[2,8,256,64]{2,3,1,0:T(8,128)S(1)}, f32[2,8,256,64]{2,3,1,0:T(8,128)}, u32[]{:S(2)}) copy-start(f32[2,8,256,64]{2,3,1,0:T(8,128)} %custom-call.2) | copy-start | bytes 3145732
  611.4 6.6 copy-start.10
  617.0 1.0 copy-start.5
  617.0 1.1 copy-start.9
  617.0 1.1 copy-start.11
  618.0 1686.2 %all-reduce.9.cloned.1.call-start = ((), (), s32[]{:S(2)}) async-start(), calls=%async_computation.1 | async-start | bytes 2097152 | tf_op jit(solution)/shard_map/psum | solution.py:163
  1223.1 100.8 %copy-start.7 = (f32[2,8,256]{2,1,0:T(8,128)}, f32[2,8,256]{2,1,0:T(8,128)S(1)}, u32[]{:S(2)}) copy-start(f32[2,8,256]{2,1,0:T(8,128)S(1)} %psum.21) | copy-start | bytes 49156
  1226.2 97.7 %copy-start.8 = (bf16[1,2,1024]{2,1,0:T(2,128)(2,1)}, bf16[1,2,1024]{2,1,0:T(2,128)(2,1)S(1)}, u32[]{:S(2)}) copy-start(bf16[1,2,1024]{2,1,0:T(2,128)(2,1)S(1)} %copy.70) | copy-start | bytes 12292
  1329.5 0.9 copy-start.1
  1331.1 0.7 copy-start.2
  1335.3 0.9 copy-start.1
  1336.9 0.7 copy-start.2
  1337.6 499.8 %copy-start.3 = (bf16[512,2,64]{0,2,1:T(8,128)(2,1)S(1)}, bf16[512,2,64]{0,2,1:T(8,128)(2,1)}, u32[]{:S(2)}) copy-start(bf16[512,2,64]{0,2,1:T(8,128)(2,1)} %get-tuple-element.444) | copy-start | bytes 393220
  1337.6 499.8 %copy-start.6 = (bf16[1024,128]{1,0:T(8,128)(2,1)S(1)}, bf16[1024,128]{1,0:T(8,128)(2,1)}, u32[]{:S(2)}) copy-start(bf16[1024,128]{1,0:T(8,128)(2,1)} %param.14) | copy-start | bytes 786436
Sparse Core Ops, SparseCore 0:
  618.1 336.3 all-reduce.6
  1836.6 467.5 all-reduce.8
where the time goes:
time: 2320 us
  blocking collectives  1780 us (77%)
  waiting for transfers between devices  464 us (20%)
  matrix products  25.4 us (1%)
    unnamed x1, blocking collectives  495 us
    pmax x1, blocking collectives, shards(): peaks = lax.pmax(local_peaks, 'seq')  488 us
    psum x1, blocking collectives, shards(): totals = lax.psum(totals, 'seq')  488 us
    psum x1, waiting for transfers between devices, shards(): weight_k, weight_v = lax.psum((weight_k, weight_v), ('seq', 'dp'))  464 us
    all_gather x1, blocking collectives, shards(): lax.all_gather(out_grad[0], 'seq', axis=0, tiled=True)  113 us
    all_gather x1, blocking collectives, shards(): queries = lax.all_gather(latent_queries, 'seq', axis=1, tiled=True)[0]  109 us
    all_gather x1, blocking collectives, shards(): lax.all_gather(attended, 'seq', axis=0, tiled=True)  91.1 us
  transfers between devices with their start and end apart: 2, of which 1 were waited for; matrix products, arithmetic and copies ran while one was open for 0% of the time, Pallas kernels for 0%

commit v1 on v0

v1 whole, which is shorter than its diff:
```python
import functools

import jax
import jax.numpy as jnp
from jax import lax
from jax.experimental import pallas as pl
from jax.experimental.pallas import tpu as pltpu
from jax.sharding import PartitionSpec as P

MESH = pl.DeviceIdType.MESH
HD = 64
BLK = 128
NZ = 16
MASKED = -1e30
F32 = jnp.float32
BF16 = jnp.bfloat16


def dot_nt(a, b):
    return lax.dot_general(a, b, (((1,), (1,)), ((), ())), preferred_element_type=F32)


def dot_nn(a, b):
    return jnp.dot(a, b, preferred_element_type=F32)


def kernel(
    dims,
    ctx_ref, bv_ref, kw_ref, vw_ref, lq_ref, og_ref,
    att_ref, dq_ref, cg_ref, wk_ref, wv_ref,
    blk, xblk, qg, dog, wg, kvx, kvr, ke, ko, ve, vo, bias,
    ctxo, ctxt, wsend, wrecv, zsend, zrecv, tmp1, tmp2, stz, sty,
    acc, dqs, dqr, dzs, dzr, dkv, dkvr, wsx, wrx, wsum, wzr, wza, wxa, gx,
    a16, ax, d16, dx,
    s_core, r_core, s_ag, r_z, r_y, r_rz, r_ry,
):
    nx, ny, T, D = dims
    rows = NZ * 16
    TT = 2 * T
    nxy = nx * ny
    me = lax.axis_index("seq")
    x = lax.axis_index("dp")
    c = lax.rem(me, 2)
    y = lax.rem(me // 2, ny)
    z = me // (2 * ny)
    oc = 1 - c
    base = pl.multiple_of((y * NZ + z) * 16, 16)

    def seq_of(zz, yy, cc):
        return (zz * ny + yy) * 2 + cc

    def core_peer():
        return (seq_of(z, y, oc), x)

    def z_peer(j):
        zt = lax.rem(z + j, NZ)
        return zt, (seq_of(zt, y, c), x)

    def y_peer(j):
        yt = lax.rem(y + j, ny)
        return yt, (seq_of(z, yt, c), x)

    def xy_peer(j):
        t = lax.rem(x * ny + y + j, nxy)
        return t, (seq_of(z, lax.rem(t, ny), c), t // ny)

    def send(src, dst, ssem, rsem, peer):
        pltpu.make_async_remote_copy(
            src_ref=src, dst_ref=dst, send_sem=ssem, recv_sem=rsem,
            device_id=peer, device_id_type=MESH,
        ).start()

    def wait(ref, sem):
        pltpu.make_async_copy(ref, ref, sem).wait()

    lane = lax.broadcasted_iota(jnp.int32, (1, 128), 1)
    lo = lane < HD

    barrier = pltpu.get_barrier_semaphore()
    pl.semaphore_signal(barrier, inc=1, device_id=core_peer(), device_id_type=MESH)

    @pl.loop(1, NZ)
    def _(j):
        pl.semaphore_signal(barrier, inc=1, device_id=z_peer(j)[1], device_id_type=MESH)

    @pl.loop(1, nxy)
    def _(j):
        pl.semaphore_signal(barrier, inc=1, device_id=xy_peer(j)[1], device_id_type=MESH)

    qrow = lq_ref[0].astype(F32) * (HD ** -0.5)
    orow = og_ref[0].astype(F32)
    for g in range(2):
        pieces = []
        for src in (qrow, orow):
            for l in range(2):
                for hp in range(4):
                    at = g * 512 + hp * 128
                    pieces.append(src[l:l + 1, at:at + 128])
        blk[g] = jnp.concatenate(pieces, axis=0).astype(BF16)

    kwf = kw_ref[...].astype(F32)
    vwf = vw_ref[...].astype(F32)
    wg[0] = jnp.where(lo, kwf, pltpu.roll(vwf, 64, 1)).astype(BF16)
    wg[1] = jnp.where(lo, pltpu.roll(kwf, 64, 1), vwf).astype(BF16)
    wcat = jnp.concatenate([wg[0], wg[1]], axis=1)

    @pl.loop(0, T // 128)
    def _(i):
        at = pl.ds(pl.multiple_of(i * 128, 128), 128)
        kv = dot_nn(ctx_ref[0, at, :], wcat).astype(BF16)
        kvx[0, at, :] = kv[:, :128]
        kvx[1, at, :] = kv[:, 128:]

    rowi = lax.broadcasted_iota(jnp.int32, (16, 128), 0)
    flags = jnp.zeros((16, 128), F32)
    for j in range(T // BLK):
        flags = jnp.where(rowi == j, jnp.where(bv_ref[0, j] > 0, 0.0, MASKED), flags)
    kvx[0, T:T + 16, :] = flags.astype(BF16)
    kvx[1, T:T + 16, :] = flags.astype(BF16)

    pl.semaphore_wait(barrier, 1 + (NZ - 1) + (nxy - 1))

    send(blk.at[oc], xblk, s_core.at[0], r_core.at[0], core_peer())
    send(kvx.at[oc], kvr, s_core.at[1], r_core.at[1], core_peer())
    send(ctx_ref.at[0], ctxo, s_core.at[2], r_core.at[2], core_peer())

    wait(xblk, r_core.at[0])
    own = blk[c].astype(F32)
    oth = xblk[...].astype(F32)
    first = jnp.where(c == 0, own, oth)
    second = jnp.where(c == 0, oth, own)
    qg[pl.ds(base, 16), :] = jnp.concatenate([first[:8], second[:8]], axis=0).astype(BF16)
    dog[pl.ds(base, 16), :] = jnp.concatenate([first[8:], second[8:]], axis=0).astype(BF16)

    for n, buf in enumerate((qg, dog)):
        @pl.loop(1, NZ)
        def _(j, n=n, buf=buf):
            zt, peer = z_peer(j)
            part = buf.at[pl.ds(base, 16), :]
            send(part, part, s_ag.at[n], r_z.at[n], peer)

    wait(kvr, r_core.at[1])
    for part in range(2):
        src = kvx.at[c] if part == 0 else kvr
        kv = src[0:T, :].astype(F32)
        swapped = pltpu.roll(kv, 64, 1)
        at = slice(part * T, part * T + T)
        ke[at, :] = jnp.where(lo, kv, 0.0).astype(BF16)
        ko[at, :] = jnp.where(lo, 0.0, swapped).astype(BF16)
        ve[at, :] = jnp.where(lo, swapped, 0.0).astype(BF16)
        vo[at, :] = jnp.where(lo, 0.0, kv).astype(BF16)
        fl = src[T:T + 16, :].astype(F32)
        for j in range(T // BLK):
            bias[:, part * T + j * BLK:part * T + (j + 1) * BLK] = fl[j:j + 1, :]

    yrows = pl.ds(pl.multiple_of(y * rows, rows), rows)

    def gather_y(n, buf):
        wait(buf.at[pl.ds(0, (NZ - 1) * 16), :], r_z.at[n])
        for j in range(1, ny):
            yt, peer = y_peer(j)
            part = buf.at[yrows, :]
            send(part, part, s_ag.at[2 + n], r_y.at[n, y], peer)

    gather_y(0, qg)

    def forward(yb, dst, slot):
        stat = jnp.zeros((8, 128), F32)
        for h in range(rows // 128):
            r0 = pl.multiple_of(yb * rows + h * 128, 128)
            q = qg[pl.ds(r0, 128), :]
            out = jnp.zeros((128, 128), F32)
            cols = jnp.zeros((128, 128), F32)
            for eo, (kr, vr) in enumerate(((ke, ve), (ko, vo))):
                s = dot_nt(q, kr[...]) + bias[...]
                m = jnp.max(s, axis=1, keepdims=True)
                p = jnp.exp(s - m)
                l = jnp.sum(p, axis=1, keepdims=True)
                out = out + dot_nn(p.astype(BF16), vr[...]) / l
                cols = jnp.where(lane == 2 * h + eo, m + jnp.log(l), cols)
            dst[slot, h * 128:(h + 1) * 128, :] = out
            stat = stat + cols.T[0:8, :]
        dst[slot, rows:rows + 8, :] = stat

    forward(y, wrecv, y)
    gather_y(1, dog)

    @pl.loop(1, ny)
    def _(j):
        yt, peer = y_peer(j)
        wait(qg.at[yrows, :], r_y.at[0, yt])
        forward(yt, wsend, yt)
        send(wsend.at[yt], wrecv.at[y], s_ag.at[4], r_ry.at[0, y], peer)

    wait(ctxo, r_core.at[2])

    @pl.loop(0, T // 128)
    def _(i):
        at = pl.ds(pl.multiple_of(i * 128, 128), 128)
        at2 = pl.ds(pl.multiple_of(T + i * 128, 128), 128)
        ctxt[:, at] = ctx_ref[0, at, :].T
        ctxt[:, at2] = ctxo[at, :].T

    for j in range(1, ny):
        yt, _ = y_peer(j)
        wait(wrecv.at[yt], r_ry.at[0, yt])

    stats = [wrecv[i, rows:rows + 8, :] for i in range(ny)]
    top = functools.reduce(jnp.maximum, stats)
    es = [jnp.exp(s - top) for s in stats]
    tot = functools.reduce(lambda a, b: a + b, es)
    inv = 1.0 / tot
    coef = jnp.concatenate(
        [e * inv for e in es] + [jnp.zeros((128 - 8 * ny, 128), F32)], axis=0
    ).T
    lse = top + jnp.log(tot)
    for h in range(rows // 128):
        w = jnp.zeros((128, 128), F32)
        for i in range(ny):
            k = i * 8 + 2 * h
            w = w + wrecv[i, h * 128:(h + 1) * 128, :] * jnp.where(lo, coef[:, k:k + 1], coef[:, k + 1:k + 2])
        zsend[8 * h:8 * h + 8, 0:16, :] = w.reshape(8, 16, 128)
    zsend[:, 16:24, :] = jnp.broadcast_to(lse[None], (NZ, 8, 128))

    @pl.loop(1, NZ)
    def _(j):
        zt, peer = z_peer(j)
        send(zsend.at[zt], zrecv.at[z], s_ag.at[5], r_rz.at[0], peer)

    zrecv[z] = zsend[z]
    wait(zrecv.at[pl.ds(0, NZ - 1)], r_rz.at[0])

    stat3 = zrecv[:, 16:24, :]
    top = jnp.max(stat3, axis=0)
    e3 = jnp.exp(stat3 - top[None])
    tot = jnp.sum(e3, axis=0)
    tmp1[...] = (e3 * (1.0 / tot)[None]).reshape(128, 128).T
    tmp2[...] = jnp.concatenate([top + jnp.log(tot), jnp.zeros((120, 128), F32)], axis=0).T
    hz = z // 8
    mine = pl.ds(pl.multiple_of(lax.rem(z, 8) * 16, 16), 16)
    ct = tmp1[mine, :]
    ct = jnp.where(hz == 0, ct, pltpu.roll(ct, 126, 1))
    lt = tmp2[mine, :]
    lt = jnp.where(hz == 0, lt, pltpu.roll(lt, 126, 1))
    att = jnp.zeros((16, 128), F32)
    for i in range(NZ):
        att = att + zrecv[i, 0:16, :] * jnp.where(lo, ct[:, 8 * i:8 * i + 1], ct[:, 8 * i + 1:8 * i + 2])
    att = att.astype(BF16).astype(F32)
    a16[0] = att[:8]
    a16[1] = att[8:]
    prod = dog[pl.ds(base, 16), :].astype(F32) * att
    delta_e = jnp.sum(jnp.where(lo, prod, 0.0), axis=1, keepdims=True)
    delta_o = jnp.sum(jnp.where(lo, 0.0, prod), axis=1, keepdims=True)
    vals = (lt[:, 0:1], lt[:, 1:2], delta_e, delta_o)
    cols = jnp.zeros((16, 128), F32)
    for k in range(4):
        cols = jnp.where(lane == 2 * k + hz, vals[k], cols)
    tmp1[...] = jnp.zeros((128, 128), F32)
    tmp1[mine, :] = cols
    stz[z] = tmp1[...].T[0:8, :]

    @pl.loop(1, NZ)
    def _(j):
        zt, peer = z_peer(j)
        send(stz.at[z], stz.at[z], s_ag.at[6], r_rz.at[1], peer)

    send(a16.at[oc], ax, s_core.at[3], r_core.at[3], core_peer())
    wait(stz.at[pl.ds(0, NZ - 1)], r_rz.at[1])
    sty[y] = jnp.sum(stz[...], axis=0)
    for j in range(1, ny):
        yt, peer = y_peer(j)
        send(sty.at[y], sty.at[y], s_ag.at[7], r_ry.at[1, y], peer)

    acc[...] = jnp.zeros((128, TT), F32)

    def backward(yb, dst, slot):
        cols = jnp.concatenate([sty[yb], jnp.zeros((120, 128), F32)], axis=0).T
        grads = [[], []]
        probs = [[], []]
        qs, os = [], []
        for h in range(rows // 128):
            r0 = pl.multiple_of(yb * rows + h * 128, 128)
            q = qg[pl.ds(r0, 128), :]
            o = dog[pl.ds(r0, 128), :]
            qs.append(q)
            os.append(o)
            out = jnp.zeros((128, 128), F32)
            for eo, (kr, vr) in enumerate(((ke, ve), (ko, vo))):
                k = 2 * eo + h
                s = dot_nt(q, kr[...]) + bias[...]
                p = jnp.exp(s - cols[:, k:k + 1])
                slopes = dot_nt(o, vr[...])
                ds = (p * (slopes - cols[:, 4 + k:5 + k])).astype(BF16)
                probs[eo].append(p.astype(BF16))
                grads[eo].append(ds)
                out = out + dot_nn(ds, kr[...])
            dst[slot, h * 128:(h + 1) * 128, :] = (out * (HD ** -0.5)).astype(BF16)
        cat = lambda parts: jnp.concatenate(parts, axis=0)
        qt = cat(qs).T
        ot = cat(os).T
        acc[0:64, :] += dot_nn(qt[:64], cat(grads[0])) + dot_nn(qt[64:], cat(grads[1]))
        acc[64:128, :] += dot_nn(ot[:64], cat(probs[0])) + dot_nn(ot[64:], cat(probs[1]))

    for j in range(1, ny):
        yt, _ = y_peer(j)
        wait(dog.at[yrows, :], r_y.at[1, yt])

    backward(y, dqr, y)

    @pl.loop(1, ny)
    def _(j):
        yt, peer = y_peer(j)
        wait(sty.at[y], r_ry.at[1, yt])
        backward(yt, dqs, yt)
        send(dqs.at[yt], dqr.at[y], s_ag.at[8], r_ry.at[2, y], peer)

    @pl.loop(0, TT // 128)
    def _(i):
        at = pl.ds(pl.multiple_of(i * 128, 128), 128)
        dkv[at, :] = acc[:, at].T.astype(BF16)

    send(dkv.at[pl.ds(T, T), :], dkvr, s_core.at[4], r_core.at[4], core_peer())

    sl = D // nxy
    mexy = x * ny + y

    @pl.loop(0, D // 256 if D >= 256 else 1)
    def _(i):
        n = min(256, D)
        g = dot_nn(ctxt[pl.ds(pl.multiple_of(i * n, n), n), :], dkv[...])
        wsx[pl.ds(i * (n // sl), n // sl)] = g.reshape(n // sl, sl, 128)

    @pl.loop(1, nxy)
    def _(j):
        t, peer = xy_peer(j)
        send(wsx.at[t], wrx.at[mexy], s_ag.at[9], r_rz.at[2], peer)

    wrx[mexy] = wsx[mexy]

    for j in range(1, ny):
        yt, _ = y_peer(j)
        wait(dqr.at[yt], r_ry.at[2, yt])
    dqy = functools.reduce(lambda a, b: a + b, [dqr[i].astype(F32) for i in range(ny)])
    dzs[...] = dqy.reshape(NZ, 16, 128).astype(BF16)

    @pl.loop(1, NZ)
    def _(j):
        zt, peer = z_peer(j)
        send(dzs.at[zt], dzr.at[z], s_ag.at[10], r_rz.at[3], peer)

    dzr[z] = dzs[z]

    wait(dkvr, r_core.at[4])

    @pl.loop(0, T // 128)
    def _(i):
        at = pl.ds(pl.multiple_of(i * 128, 128), 128)
        g = dot_nt(dkv[at, :], wg[c]) + dot_nt(dkvr[at, :], wg[oc])
        cg_ref[0, at, :] = g.astype(BF16)

    wait(dzr.at[pl.ds(0, NZ - 1)], r_rz.at[3])
    dq = jnp.sum(dzr[...].astype(F32), axis=0)
    d16[0] = dq[:8]
    d16[1] = dq[8:]
    send(d16.at[oc], dx, s_core.at[5], r_core.at[5], core_peer())

    wait(wrx.at[pl.ds(0, nxy - 1)], r_rz.at[2])
    wsum[...] = jnp.sum(wrx[...], axis=0).reshape(8, sl // 8, 128)

    @pl.loop(1, NZ)
    def _(j):
        zt, peer = z_peer(j)
        send(wsum.at[zt // 2], wzr.at[z], s_ag.at[11], r_rz.at[4], peer)

    wzr[z] = wsum[z // 2]

    def own_rows(mine8, other8):
        f8 = jnp.where(c == 0, mine8, other8)
        s8 = jnp.where(c == 0, other8, mine8)
        lines = []
        for l in range(2):
            lines.append(jnp.concatenate(
                [g8[4 * l + hp:4 * l + hp + 1, :] for g8 in (f8, s8) for hp in range(4)], axis=1))
        return jnp.concatenate(lines, axis=0).astype(BF16)

    wait(ax, r_core.at[3])
    att_ref[0] = own_rows(a16[c], ax[...])
    wait(dx, r_core.at[5])
    dq_ref[0] = own_rows(d16[c], dx[...])

    wait(wzr.at[pl.ds(0, NZ - 1)], r_rz.at[4])
    wza[z // 2] = jnp.sum(wzr[...], axis=0)

    @pl.loop(1, NZ // 2)
    def _(j):
        zt, peer = z_peer(2 * j)
        send(wza.at[z // 2], wza.at[z // 2], s_ag.at[12], r_rz.at[5], peer)

    wait(wza.at[pl.ds(0, NZ // 2 - 1)], r_rz.at[5])
    wxa[mexy] = wza[...].reshape(sl, 128)

    @pl.loop(1, nxy)
    def _(j):
        t, peer = xy_peer(j)
        send(wxa.at[mexy], wxa.at[mexy], s_ag.at[13], r_rz.at[6], peer)

    wait(wxa.at[pl.ds(0, nxy - 1)], r_rz.at[6])
    send(wxa, gx, s_core.at[6], r_core.at[6], core_peer())
    wait(gx, r_core.at[6])
    ga = wxa[...].reshape(D, 128)
    gb = gx[...].reshape(D, 128)
    g0 = jnp.where(c == 0, ga, gb)
    g1 = jnp.where(c == 0, gb, ga)
    wk_ref[...] = jnp.where(lo, g0, pltpu.roll(g1, 64, 1))
    wv_ref[...] = jnp.where(lo, pltpu.roll(g0, 64, 1), g1)

    wait(xblk, s_core.at[0])
    wait(kvr, s_core.at[1])
    wait(ctxo, s_core.at[2])
    wait(ax, s_core.at[3])
    wait(dkvr, s_core.at[4])
    wait(dx, s_core.at[5])
    wait(gx, s_core.at[6])
    for n in range(2):
        wait(qg.at[pl.ds(0, (NZ - 1) * 16), :], s_ag.at[n])
        wait(qg.at[pl.ds(0, (ny - 1) * rows), :], s_ag.at[2 + n])
    wait(wrecv.at[pl.ds(0, ny - 1)], s_ag.at[4])
    wait(zrecv.at[pl.ds(0, NZ - 1)], s_ag.at[5])
    wait(stz.at[pl.ds(0, NZ - 1)], s_ag.at[6])
    wait(sty.at[pl.ds(0, ny - 1)], s_ag.at[7])
    wait(dqr.at[pl.ds(0, ny - 1)], s_ag.at[8])
    wait(wrx.at[pl.ds(0, nxy - 1)], s_ag.at[9])
    wait(dzr.at[pl.ds(0, NZ - 1)], s_ag.at[10])
    wait(wzr.at[pl.ds(0, NZ - 1)], s_ag.at[11])
    wait(wza.at[pl.ds(0, NZ // 2 - 1)], s_ag.at[12])
    wait(wxa.at[pl.ds(0, nxy - 1)], s_ag.at[13])


def solution(mesh):
    ny = mesh.shape["seq"] // (2 * NZ)
    nx = mesh.shape["dp"]

    def step(context, block_valid, key_weight, value_weight, latent_queries, out_grad):
        T, D = context.shape[1:]
        rows = NZ * 16
        nr = ny * rows
        nxy = nx * ny
        sl = D // nxy
        vm = lambda shape, dtype=F32: pltpu.VMEM(shape, dtype)
        vmem = pl.BlockSpec(memory_space=pltpu.VMEM)
        smem = pl.BlockSpec(memory_space=pltpu.SMEM)
        dma = pltpu.SemaphoreType.DMA
        return pl.pallas_call(
            functools.partial(kernel, (nx, ny, T, D)),
            out_shape=(
                jax.ShapeDtypeStruct(latent_queries.shape, BF16),
                jax.ShapeDtypeStruct(latent_queries.shape, BF16),
                jax.ShapeDtypeStruct(context.shape, BF16),
                jax.ShapeDtypeStruct((D, 128), F32),
                jax.ShapeDtypeStruct((D, 128), F32),
            ),
            in_specs=[vmem, smem, vmem, vmem, vmem, vmem],
            out_specs=(vmem,) * 5,
            scratch_shapes=[
                vm((2, 16, 128), BF16), vm((16, 128), BF16),
                vm((nr, 128), BF16), vm((nr, 128), BF16),
                vm((2, D, 128), BF16),
                vm((2, T + 16, 128), BF16), vm((T + 16, 128), BF16),
                vm((2 * T, 128), BF16), vm((2 * T, 128), BF16),
                vm((2 * T, 128), BF16), vm((2 * T, 128), BF16),
                vm((1, 2 * T)),
                vm((T, D), BF16), vm((D, 2 * T), BF16),
                vm((ny, rows + 8, 128)), vm((ny, rows + 8, 128)),
                vm((NZ, 24, 128)), vm((NZ, 24, 128)),
                vm((128, 128)), vm((128, 128)),
                vm((NZ, 8, 128)), vm((ny, 8, 128)),
                vm((128, 2 * T)),
                vm((ny, rows, 128), BF16), vm((ny, rows, 128), BF16),
                vm((NZ, 16, 128), BF16), vm((NZ, 16, 128), BF16),
                vm((2 * T, 128), BF16), vm((T, 128), BF16),
                vm((nxy, sl, 128)), vm((nxy, sl, 128)),
                vm((8, sl // 8, 128)), vm((NZ, sl // 8, 128)), vm((8, sl // 8, 128)),
                vm((nxy, sl, 128)), vm((nxy, sl, 128)),
                vm((2, 8, 128)), vm((8, 128)), vm((2, 8, 128)), vm((8, 128)),
                dma((7,)), dma((7,)), dma((14,)), dma((2,)), dma((2, ny)),
                dma((7,)), dma((3, ny)),
            ],
            compiler_params=pltpu.CompilerParams(
                collective_id=0, has_side_effects=True, vmem_limit_bytes=50 * 1024 * 1024
            ),
        )(context, block_valid, key_weight, value_weight, latent_queries, out_grad)

    in_specs = (
        P("dp", "seq", None), P("dp", "seq"), P(), P(),
        P("dp", "seq", None), P("dp", "seq", None),
    )
    out_specs = (P("dp", "seq", None), P("dp", "seq", None), P("dp", "seq", None), P(), P())
    return jax.shard_map(step, mesh=mesh, in_specs=in_specs, out_specs=out_specs, check_vma=False)
```

time: 2320 us -> 124 us (0.05)
  blocking collectives: 1780 us -> 0 us
  waiting for transfers between devices: 464 us -> 0 us
  Pallas kernels: 0 us -> 114 us
  matrix products: 25.4 us -> 0 us
    unnamed x1 -> x0, blocking collectives: 495 us -> none
    pmax x1 -> x0, blocking collectives: 488 us -> none  [shards(): peaks = lax.pmax(local_peaks, 'seq')]
    psum x1 -> x0, blocking collectives: 488 us -> none  [shards(): totals = lax.psum(totals, 'seq')]
    psum x1 -> x0, waiting for transfers between devices: 464 us -> none  [shards(): weight_k, weight_v = lax.psum((weight_k, weight_v), ('seq', 'dp'))]
    all_gather x3 -> x0, blocking collectives: 313 us -> none  [the longest x1 113 us: shards(): lax.all_gather(out_grad[0], 'seq', axis=0, tiled=True)]
    pallas_call x0 -> x1, Pallas kernels: none -> 114 us  [step(): pl.pallas_call(functools.partial(kernel, (nx, ny, T, D)), out_shape=(jax....]
    dot_general x22 -> x0, matrix products: 25.4 us -> none  [the longest x6 8.45 us: block_scores(): jnp.einsum('cgld,kcd->cglk', grouped, key_part, preferred_element_type=jn...]
  transfers between devices with their start and end apart: 2 -> 0, of which waited for: 1 -> 0; matrix products, arithmetic and copies ran while one was open for 0% -> 0% of each run, Pallas kernels for 0% -> 0%
where the time goes in v1:
time: 124 us
  Pallas kernels  114 us (92%)
  local copies, waits for them, and re-layouts  8.89 us (7%)
    pallas_call x1, Pallas kernels, step(): pl.pallas_call(functools.partial(kernel, (nx, ny, T, D)), out_shape=(jax....  114 us
    unnamed x17, local copies, waits for them, and re-layouts  8.89 us

profile of v1, /device:TPU:1, one launch (start us, length us, event | category | flops | bytes accessed | tf_op | source)
XLA Modules:
  0.0 124.0 jit_solution(10620933104939399938)
XLA Ops:
  0.6 0.0 copy-start
  0.6 1.2 copy-done
  1.9 0.0 copy-start.1
  1.9 0.9 copy-done.1
  2.8 0.0 copy-start.2
  2.8 0.9 copy-done.2
  3.8 0.0 copy-start.3
  3.8 0.7 copy-done.3
  4.4 0.0 copy-start.4
  4.4 0.7 copy-done.4
  5.1 0.0 copy-start.5
  5.1 0.7 copy-done.5
  5.8 114.4 %shard_map.101 = (bf16[1,2,1024]{2,1,0:T(2,128)(2,1)S(1)}, bf16[1,2,1024]{2,1,0:T(2,128)(2,1)S(1)}, bf16[1,512,1024]{2,1,0:T(8,128)(2,1)S(1)}, f32[1024,128]{1,0:T(8,128)S(1)}, f32[1024,128]{1,0:T(8,128)S(1)}) custom-call(bf16[1,512,1024]{2,1,0:T(8,128)(2,1)S(1)} %copy-done, s32[1,4]{1,0:T(1,128)S(1)} %copy-done.5, bf16[1024,128]{1,0:T(8,128)(2,1)S(1)} %copy-done.1, ...), custom_call_target="tpu_custom_call" | custom-call | tf_op jit(solution)/shard_map/pallas_call | solution.py:453
  120.2 0.6 copy.16
  120.8 0.6 copy.17
  121.4 1.0 copy.18
  122.4 0.8 copy.19
  123.2 0.8 copy.20
Async XLA Ops:
  0.6 1.2 copy-start
  1.9 0.9 copy-start.1
  2.8 0.9 copy-start.2
  3.8 0.7 copy-start.3
  4.4 0.7 copy-start.4
  5.1 0.7 copy-start.5

commit v2 on v1

v2 whole, which is shorter than its diff:
```python
import functools

import jax
import jax.numpy as jnp
from jax import lax
from jax.experimental import pallas as pl
from jax.experimental.pallas import tpu as pltpu
from jax.sharding import PartitionSpec as P

MESH = pl.DeviceIdType.MESH
HD = 64
BLK = 128
NZ = 16
MASKED = -1e30
F32 = jnp.float32
BF16 = jnp.bfloat16


def dot_nt(a, b):
    return lax.dot_general(a, b, (((1,), (1,)), ((), ())), preferred_element_type=F32)


def dot_nn(a, b):
    return jnp.dot(a, b, preferred_element_type=F32)


def combine(tiles):
    head = lax.broadcasted_iota(jnp.int32, (8, 128), 0) < 4
    top = functools.reduce(jnp.maximum, tiles)
    tot = jnp.zeros((8, 128), F32)
    mean = jnp.zeros((8, 128), F32)
    for t in tiles:
        e = jnp.exp(jnp.where(head, t - top, MASKED))
        e = e + pltpu.roll(e, 4, 0)
        tot = tot + e
        mean = mean + e * t
    return jnp.where(head, top + jnp.log(tot), mean / tot)


def kernel(
    dims,
    ctx_hbm, bv_ref, kw_hbm, vw_hbm, lq_hbm, og_hbm,
    att_ref, dq_ref, cg_ref, wk_ref, wv_ref,
    ctx, kw, vw, lq, og,
    blk, xblk, qg, dog, wg, kvx, kvr, ke, ko, ve, vo, bias,
    ctxo, ctxt, wsend, wrecv, sys_, syr, stz, sty, zsend, zrecv,
    acc, dqs, dqr, dzs, dzr, dkv, dkvr, wsx, wrx, wps, wpr, wza, wxa, gx,
    a16, ax, d16, dx,
    s_in, s_core, r_core, s_ag, r_qz, r_y, r_rz, r_ry,
):
    nx, ny, T, D = dims
    rows = NZ * 16
    TT = 2 * T
    nxy = nx * ny
    me = lax.axis_index("seq")
    x = lax.axis_index("dp")
    c = lax.rem(me, 2)
    y = lax.rem(me // 2, ny)
    z = me // (2 * ny)
    oc = 1 - c
    base = pl.multiple_of((y * NZ + z) * 16, 16)
    yrows = pl.ds(pl.multiple_of(y * rows, rows), rows)
    mexy = x * ny + y

    def seq_of(zz, yy, cc):
        return (zz * ny + yy) * 2 + cc

    def core_peer():
        return (seq_of(z, y, oc), x)

    def z_peer(j):
        zt = lax.rem(z + j, NZ)
        return zt, (seq_of(zt, y, c), x)

    def y_peer(j):
        yt = lax.rem(y + j, ny)
        return yt, (seq_of(z, yt, c), x)

    def xy_peer(j):
        t = lax.rem(mexy + j, nxy)
        return t, (seq_of(z, lax.rem(t, ny), c), t // ny)

    def spread(k, n):
        odd = lax.rem(k, 2)
        return lax.rem(odd * ((k + 1) // 2) + (1 - odd) * (n - k // 2), n)

    def send(src, dst, ssem, rsem, peer):
        pltpu.make_async_remote_copy(
            src_ref=src, dst_ref=dst, send_sem=ssem, recv_sem=rsem,
            device_id=peer, device_id_type=MESH,
        ).start()

    def wait(ref, sem):
        pltpu.make_async_copy(ref, ref, sem).wait()

    def to_z(fn):
        @pl.loop(0, NZ - 1)
        def _(k):
            fn(*z_peer(NZ // 2 + spread(k, NZ)))

    lane = lax.broadcasted_iota(jnp.int32, (1, 128), 1)
    lo = lane < HD

    barrier = pltpu.get_barrier_semaphore()

    @pl.loop(0, NZ - 1)
    def _(k):
        _, peer = z_peer(NZ // 2 + spread(k, NZ))
        pl.semaphore_signal(barrier, inc=1, device_id=peer, device_id_type=MESH)

    @pl.loop(1, nxy)
    def _(j):
        pl.semaphore_signal(barrier, inc=1, device_id=xy_peer(j)[1], device_id_type=MESH)

    pl.semaphore_signal(barrier, inc=1, device_id=core_peer(), device_id_type=MESH)

    loads = [
        pltpu.make_async_copy(src, dst, s_in.at[i])
        for i, (src, dst) in enumerate(
            ((lq_hbm, lq), (og_hbm, og), (kw_hbm, kw), (vw_hbm, vw), (ctx_hbm.at[0], ctx))
        )
    ]
    for load in loads:
        load.start()

    loads[0].wait()
    loads[1].wait()
    qrow = lq[0].astype(F32) * (HD ** -0.5)
    orow = og[0].astype(F32)
    for g in range(2):
        pieces = []
        for src in (qrow, orow):
            for l in range(2):
                for hp in range(4):
                    at = g * 512 + hp * 128
                    pieces.append(src[l:l + 1, at:at + 128])
        blk[g] = jnp.concatenate(pieces, axis=0).astype(BF16)

    loads[2].wait()
    loads[3].wait()
    kwf = kw[...].astype(F32)
    vwf = vw[...].astype(F32)
    wg[0] = jnp.where(lo, kwf, pltpu.roll(vwf, 64, 1)).astype(BF16)
    wg[1] = jnp.where(lo, pltpu.roll(kwf, 64, 1), vwf).astype(BF16)
    wcat = jnp.concatenate([wg[0], wg[1]], axis=1)
    loads[4].wait()

    @pl.loop(0, T // 128)
    def _(i):
        at = pl.ds(pl.multiple_of(i * 128, 128), 128)
        kv = dot_nn(ctx[at, :], wcat).astype(BF16)
        kvx[0, at, :] = kv[:, :128]
        kvx[1, at, :] = kv[:, 128:]

    rowi = lax.broadcasted_iota(jnp.int32, (16, 128), 0)
    flags = jnp.zeros((16, 128), F32)
    for j in range(T // BLK):
        flags = jnp.where(rowi == j, jnp.where(bv_ref[0, j] > 0, 0.0, MASKED), flags)
    kvx[0, T:T + 16, :] = flags.astype(BF16)
    kvx[1, T:T + 16, :] = flags.astype(BF16)

    @pl.loop(0, T // 128)
    def _(i):
        at = pl.ds(pl.multiple_of(i * 128, 128), 128)
        ctxt[:, at] = ctx[at, :].T

    pl.semaphore_wait(barrier, 1 + (NZ - 1) + (nxy - 1))

    send(blk.at[oc], xblk, s_core.at[0], r_core.at[0], core_peer())
    send(kvx.at[oc], kvr, s_core.at[1], r_core.at[1], core_peer())

    wait(xblk, r_core.at[0])
    own = blk[c].astype(F32)
    oth = xblk[...].astype(F32)
    first = jnp.where(c == 0, own, oth)
    second = jnp.where(c == 0, oth, own)
    qg[pl.ds(base, 16), :] = jnp.concatenate([first[:8], second[:8]], axis=0).astype(BF16)
    dog[pl.ds(base, 16), :] = jnp.concatenate([first[8:], second[8:]], axis=0).astype(BF16)

    qown = qg.at[pl.ds(base, 16), :]
    oown = dog.at[pl.ds(base, 16), :]
    to_z(lambda zt, peer: send(qown, qown, s_ag.at[0], r_qz.at[z], peer))
    to_z(lambda zt, peer: send(oown, oown, s_ag.at[1], r_rz.at[0], peer))
    send(ctx, ctxo, s_core.at[2], r_core.at[2], core_peer())

    wait(kvr, r_core.at[1])
    for part in range(2):
        src = kvx.at[c] if part == 0 else kvr
        kv = src[0:T, :].astype(F32)
        swapped = pltpu.roll(kv, 64, 1)
        at = slice(part * T, part * T + T)
        ke[at, :] = jnp.where(lo, kv, 0.0).astype(BF16)
        ko[at, :] = jnp.where(lo, 0.0, swapped).astype(BF16)
        ve[at, :] = jnp.where(lo, swapped, 0.0).astype(BF16)
        vo[at, :] = jnp.where(lo, 0.0, kv).astype(BF16)
        fl = src[T:T + 16, :].astype(F32)
        for j in range(T // BLK):
            bias[:, part * T + j * BLK:part * T + (j + 1) * BLK] = fl[j:j + 1, :]

    @pl.loop(0, NZ)
    def _(k):
        zs = lax.rem(z + spread(k, NZ), NZ)
        part = qg.at[pl.ds(pl.multiple_of((y * NZ + zs) * 16, 16), 16), :]

        @pl.when(k > 0)
        def _():
            wait(part, r_qz.at[zs])

        for j in range(1, ny):
            send(part, part, s_ag.at[2], r_y.at[0, y], y_peer(j)[1])

    wait(dog.at[pl.ds(0, (NZ - 1) * 16), :], r_rz.at[0])
    for j in range(1, ny):
        part = dog.at[yrows, :]
        send(part, part, s_ag.at[3], r_y.at[1, y], y_peer(j)[1])

    def forward(yb, wait_o, dst, sdst):
        outs, logs = [], []
        for h in range(rows // 128):
            r0 = pl.multiple_of(yb * rows + h * 128, 128)
            q = qg[pl.ds(r0, 128), :]
            out = jnp.zeros((128, 128), F32)
            for kr, vr in ((ke, ve), (ko, vo)):
                s = dot_nt(q, kr[...]) + bias[...]
                m = jnp.max(s, axis=1, keepdims=True)
                p = jnp.exp(s - m)
                l = jnp.sum(p, axis=1, keepdims=True)
                out = out + dot_nn(p.astype(BF16), vr[...]) / l
                logs.append(m + jnp.log(l))
            dst[yb, h * 128:(h + 1) * 128, :] = out.astype(BF16)
            outs.append(out)
        wait_o()
        stat = jnp.zeros((8, 128), F32)
        for h in range(rows // 128):
            r0 = pl.multiple_of(yb * rows + h * 128, 128)
            prod = outs[h] * dog[pl.ds(r0, 128), :].astype(F32)
            even = jnp.sum(jnp.where(lo, prod, 0.0), axis=1, keepdims=True)
            odd = jnp.sum(jnp.where(lo, 0.0, prod), axis=1, keepdims=True)
            cols = jnp.zeros((128, 128), F32)
            for k, val in ((0, logs[2 * h]), (1, logs[2 * h + 1]), (4, even), (5, odd)):
                cols = jnp.where(lane == 2 * h + k, val, cols)
            stat = stat + cols.T[0:8, :]
        sdst[yb] = stat

    forward(y, lambda: None, wrecv, syr)

    @pl.loop(1, ny)
    def _(j):
        yt, peer = y_peer(j)
        wait(qg.at[yrows, :], r_y.at[0, yt])
        forward(yt, lambda: wait(dog.at[yrows, :], r_y.at[1, yt]), wsend, sys_)
        send(sys_.at[yt], syr.at[y], s_ag.at[4], r_ry.at[0, y], peer)

    for j in range(1, ny):
        yt, peer = y_peer(j)
        send(wsend.at[yt], wrecv.at[y], s_ag.at[5], r_ry.at[1, y], peer)

    for j in range(1, ny):
        yt, _ = y_peer(j)
        wait(syr.at[yt], r_ry.at[0, yt])
    stz[z] = combine([syr[i] for i in range(ny)])
    to_z(lambda zt, peer: send(stz.at[z], stz.at[z], s_ag.at[6], r_rz.at[1], peer))

    wait(ctxo, r_core.at[2])

    @pl.loop(0, T // 128)
    def _(i):
        at = pl.ds(pl.multiple_of(i * 128, 128), 128)
        at2 = pl.ds(pl.multiple_of(T + i * 128, 128), 128)
        ctxt[:, at2] = ctxo[at, :].T

    acc[...] = jnp.zeros((128, TT), F32)
    wait(stz.at[pl.ds(0, NZ - 1)], r_rz.at[1])
    sty[y] = combine([stz[i] for i in range(NZ)])
    for j in range(1, ny):
        send(sty.at[y], sty.at[y], s_ag.at[7], r_ry.at[2, y], y_peer(j)[1])

    def backward(yb, dst):
        cols = jnp.concatenate([sty[yb], jnp.zeros((120, 128), F32)], axis=0).T
        grads = [[], []]
        probs = [[], []]
        qs, os = [], []
        for h in range(rows // 128):
            r0 = pl.multiple_of(yb * rows + h * 128, 128)
            q = qg[pl.ds(r0, 128), :]
            o = dog[pl.ds(r0, 128), :]
            qs.append(q)
            os.append(o)
            out = jnp.zeros((128, 128), F32)
            for eo, (kr, vr) in enumerate(((ke, ve), (ko, vo))):
                k = 2 * h + eo
                s = dot_nt(q, kr[...]) + bias[...]
                p = jnp.exp(s - cols[:, k:k + 1])
                slopes = dot_nt(o, vr[...])
                ds = (p * (slopes - cols[:, 4 + k:5 + k])).astype(BF16)
                probs[eo].append(p.astype(BF16))
                grads[eo].append(ds)
                out = out + dot_nn(ds, kr[...])
            dst[yb, h * 128:(h + 1) * 128, :] = (out * (HD ** -0.5)).astype(BF16)
        cat = lambda parts: jnp.concatenate(parts, axis=0)
        qt = cat(qs).T
        ot = cat(os).T
        acc[0:64, :] += dot_nn(qt[:64], cat(grads[0])) + dot_nn(qt[64:], cat(grads[1]))
        acc[64:128, :] += dot_nn(ot[:64], cat(probs[0])) + dot_nn(ot[64:], cat(probs[1]))

    backward(y, dqr)

    for j in range(1, ny):
        yt, _ = y_peer(j)
        wait(wrecv.at[yt], r_ry.at[1, yt])
    full = sty[y]
    coef = jnp.concatenate(
        [jnp.exp(jnp.minimum(syr[i] - full, 0.0)) for i in range(ny)]
        + [jnp.zeros((128 - 8 * ny, 128), F32)], axis=0
    ).T
    for h in range(rows // 128):
        w = jnp.zeros((128, 128), F32)
        for i in range(ny):
            k = i * 8 + 2 * h
            w = w + wrecv[i, h * 128:(h + 1) * 128, :].astype(F32) * jnp.where(
                lo, coef[:, k:k + 1], coef[:, k + 1:k + 2])
        zsend[8 * h:8 * h + 8] = w.reshape(8, 16, 128).astype(BF16)
    to_z(lambda zt, peer: send(zsend.at[zt], zrecv.at[z], s_ag.at[8], r_rz.at[2], peer))
    zrecv[z] = zsend[z]

    @pl.loop(1, ny)
    def _(j):
        yt, peer = y_peer(j)
        wait(sty.at[y], r_ry.at[2, yt])
        backward(yt, dqs)
        send(dqs.at[yt], dqr.at[y], s_ag.at[9], r_ry.at[3, y], peer)

    @pl.loop(0, TT // 128)
    def _(i):
        at = pl.ds(pl.multiple_of(i * 128, 128), 128)
        dkv[at, :] = acc[:, at].T.astype(BF16)

    send(dkv.at[pl.ds(T, T), :], dkvr, s_core.at[4], r_core.at[4], core_peer())

    sl = D // nxy
    n = min(256, D)

    @pl.loop(0, D // n)
    def _(i):
        g = dot_nn(ctxt[pl.ds(pl.multiple_of(i * n, n), n), :], dkv[...])
        wsx[pl.ds(i * (n // sl), n // sl)] = g.reshape(n // sl, sl, 128).astype(BF16)

    @pl.loop(1, nxy)
    def _(j):
        t, peer = xy_peer(j)
        send(wsx.at[t], wrx.at[mexy], s_ag.at[10], r_rz.at[3], peer)

    wrx[mexy] = wsx[mexy]

    for j in range(1, ny):
        yt, _ = y_peer(j)
        wait(dqr.at[yt], r_ry.at[3, yt])
    dqy = functools.reduce(lambda a, b: a + b, [dqr[i].astype(F32) for i in range(ny)])
    dzs[...] = dqy.reshape(NZ, 16, 128).astype(BF16)
    to_z(lambda zt, peer: send(dzs.at[zt], dzr.at[z], s_ag.at[11], r_rz.at[4], peer))
    dzr[z] = dzs[z]

    wait(wrx.at[pl.ds(0, nxy - 1)], r_rz.at[3])
    wps[...] = jnp.sum(wrx[...].astype(F32), axis=0)
    pair = (seq_of(z + 1 - 2 * lax.rem(z, 2), y, c), x)
    send(wps, wpr, s_core.at[7], r_core.at[7], pair)

    wait(zrecv.at[pl.ds(0, NZ - 1)], r_rz.at[2])
    att = jnp.sum(zrecv[...].astype(F32), axis=0)
    a16[0] = att[:8]
    a16[1] = att[8:]
    send(a16.at[oc], ax, s_core.at[3], r_core.at[3], core_peer())

    wait(wpr, r_core.at[7])
    wza[z // 2] = (wps[...] + wpr[...]).astype(BF16)

    @pl.loop(0, NZ // 2 - 1)
    def _(k):
        zt, peer = z_peer(NZ // 2 + 2 * spread(k, NZ // 2))
        send(wza.at[z // 2], wza.at[z // 2], s_ag.at[12], r_rz.at[5], peer)

    wait(dkvr, r_core.at[4])

    @pl.loop(0, T // 128)
    def _(i):
        at = pl.ds(pl.multiple_of(i * 128, 128), 128)
        g = dot_nt(dkv[at, :], wg[c]) + dot_nt(dkvr[at, :], wg[oc])
        cg_ref[0, at, :] = g.astype(BF16)

    wait(dzr.at[pl.ds(0, NZ - 1)], r_rz.at[4])
    dq = jnp.sum(dzr[...].astype(F32), axis=0)
    d16[0] = dq[:8]
    d16[1] = dq[8:]
    send(d16.at[oc], dx, s_core.at[5], r_core.at[5], core_peer())

    wait(wza.at[pl.ds(0, NZ // 2 - 1)], r_rz.at[5])
    wxa[mexy] = jnp.sum(wza[...].astype(F32), axis=0).astype(BF16)

    @pl.loop(1, nxy)
    def _(j):
        t, peer = xy_peer(j)
        send(wxa.at[mexy], wxa.at[mexy], s_ag.at[13], r_rz.at[6], peer)

    def own_rows(mine8, other8):
        f8 = jnp.where(c == 0, mine8, other8)
        s8 = jnp.where(c == 0, other8, mine8)
        lines = []
        for l in range(2):
            lines.append(jnp.concatenate(
                [g8[4 * l + hp:4 * l + hp + 1, :] for g8 in (f8, s8) for hp in range(4)], axis=1))
        return jnp.concatenate(lines, axis=0).astype(BF16)

    wait(ax, r_core.at[3])
    att_ref[0] = own_rows(a16[c], ax[...])
    wait(dx, r_core.at[5])
    dq_ref[0] = own_rows(d16[c], dx[...])

    wait(xblk, s_core.at[0])
    wait(kvr, s_core.at[1])
    wait(ctxo, s_core.at[2])
    wait(ax, s_core.at[3])
    wait(dkvr, s_core.at[4])
    wait(dx, s_core.at[5])
    wait(wpr, s_core.at[7])
    for i in range(2):
        wait(qg.at[pl.ds(0, (NZ - 1) * 16), :], s_ag.at[i])
        wait(qg.at[pl.ds(0, (ny - 1) * rows), :], s_ag.at[2 + i])
    wait(syr.at[pl.ds(0, ny - 1)], s_ag.at[4])
    wait(wrecv.at[pl.ds(0, ny - 1)], s_ag.at[5])
    wait(stz.at[pl.ds(0, NZ - 1)], s_ag.at[6])
    wait(sty.at[pl.ds(0, ny - 1)], s_ag.at[7])
    wait(zrecv.at[pl.ds(0, NZ - 1)], s_ag.at[8])
    wait(dqr.at[pl.ds(0, ny - 1)], s_ag.at[9])
    wait(wrx.at[pl.ds(0, nxy - 1)], s_ag.at[10])
    wait(dzr.at[pl.ds(0, NZ - 1)], s_ag.at[11])
    wait(wza.at[pl.ds(0, NZ // 2 - 1)], s_ag.at[12])

    wait(wxa.at[pl.ds(0, nxy - 1)], r_rz.at[6])
    send(wxa, gx, s_core.at[6], r_core.at[6], core_peer())
    wait(wxa.at[pl.ds(0, nxy - 1)], s_ag.at[13])
    wait(gx, r_core.at[6])
    ga = wxa[...].astype(F32).reshape(D, 128)
    gb = gx[...].astype(F32).reshape(D, 128)
    g0 = jnp.where(c == 0, ga, gb)
    g1 = jnp.where(c == 0, gb, ga)
    wk_ref[...] = jnp.where(lo, g0, pltpu.roll(g1, 64, 1))
    wv_ref[...] = jnp.where(lo, pltpu.roll(g0, 64, 1), g1)
    wait(gx, s_core.at[6])


def store(*refs):
    n = len(refs) // 2
    sems = refs[-1]
    copies = [pltpu.make_async_copy(refs[i], refs[n + i], sems.at[i]) for i in range(n)]
    for copy in copies:
        copy.start()
    for copy in copies:
        copy.wait()


def solution(mesh):
    ny = mesh.shape["seq"] // (2 * NZ)
    nx = mesh.shape["dp"]

    def step(context, block_valid, key_weight, value_weight, latent_queries, out_grad):
        T, D = context.shape[1:]
        rows = NZ * 16
        nr = ny * rows
        nxy = nx * ny
        sl = D // nxy
        vm = lambda shape, dtype=F32: pltpu.VMEM(shape, dtype)
        vmem = pl.BlockSpec(memory_space=pltpu.VMEM)
        smem = pl.BlockSpec(memory_space=pltpu.SMEM)
        hbm = pl.BlockSpec(memory_space=pltpu.HBM)
        dma = pltpu.SemaphoreType.DMA
        shapes = (
            jax.ShapeDtypeStruct(latent_queries.shape, BF16),
            jax.ShapeDtypeStruct(latent_queries.shape, BF16),
            jax.ShapeDtypeStruct(context.shape, BF16),
            jax.ShapeDtypeStruct((D, 128), F32),
            jax.ShapeDtypeStruct((D, 128), F32),
        )
        results = pl.pallas_call(
            functools.partial(kernel, (nx, ny, T, D)),
            out_shape=tuple(pltpu.VMEM(q.shape, q.dtype) for q in shapes),
            in_specs=[hbm, smem, hbm, hbm, hbm, hbm],
            out_specs=(vmem,) * 5,
            scratch_shapes=[
                vm((T, D), BF16), vm((D, 128), BF16), vm((D, 128), BF16),
                vm(latent_queries.shape, BF16), vm(latent_queries.shape, BF16),
                vm((2, 16, 128), BF16), vm((16, 128), BF16),
                vm((nr, 128), BF16), vm((nr, 128), BF16),
                vm((2, D, 128), BF16),
                vm((2, T + 16, 128), BF16), vm((T + 16, 128), BF16),
                vm((2 * T, 128), BF16), vm((2 * T, 128), BF16),
                vm((2 * T, 128), BF16), vm((2 * T, 128), BF16),
                vm((1, 2 * T)),
                vm((T, D), BF16), vm((D, 2 * T), BF16),
                vm((ny, rows, 128), BF16), vm((ny, rows, 128), BF16),
                vm((ny, 8, 128)), vm((ny, 8, 128)), vm((NZ, 8, 128)), vm((ny, 8, 128)),
                vm((NZ, 16, 128), BF16), vm((NZ, 16, 128), BF16),
                vm((128, 2 * T)),
                vm((ny, rows, 128), BF16), vm((ny, rows, 128), BF16),
                vm((NZ, 16, 128), BF16), vm((NZ, 16, 128), BF16),
                vm((2 * T, 128), BF16), vm((T, 128), BF16),
                vm((nxy, sl, 128), BF16), vm((nxy, sl, 128), BF16),
                vm((sl, 128)), vm((sl, 128)),
                vm((NZ // 2, sl, 128), BF16),
                vm((nxy, sl, 128), BF16), vm((nxy, sl, 128), BF16),
                vm((2, 8, 128)), vm((8, 128)), vm((2, 8, 128)), vm((8, 128)),
                dma((5,)), dma((8,)), dma((8,)), dma((14,)), dma((NZ,)), dma((2, ny)),
                dma((7,)), dma((4, ny)),
            ],
            compiler_params=pltpu.CompilerParams(
                collective_id=0, has_side_effects=True, vmem_limit_bytes=60 * 1024 * 1024
            ),
        )(context, block_valid, key_weight, value_weight, latent_queries, out_grad)
        return tuple(pl.pallas_call(
            store,
            out_shape=shapes,
            in_specs=[vmem] * 5,
            out_specs=(hbm,) * 5,
            scratch_shapes=[dma((5,))],
            compiler_params=pltpu.CompilerParams(vmem_limit_bytes=1024 * 1024),
        )(*results))

    in_specs = (
        P("dp", "seq", None), P("dp", "seq"), P(), P(),
        P("dp", "seq", None), P("dp", "seq", None),
    )
    out_specs = (P("dp", "seq", None), P("dp", "seq", None), P("dp", "seq", None), P(), P())
    return jax.shard_map(step, mesh=mesh, in_specs=in_specs, out_specs=out_specs, check_vma=False)
```

time: 124 us -> 83.7 us (0.68)
  Pallas kernels: 114 us -> 82.9 us
  local copies, waits for them, and re-layouts: 8.89 us -> 0 us
    pallas_call x1 -> x2, Pallas kernels: 114 us -> 82.9 us  [the longest x1 81.5 us: step(): pl.pallas_call(functools.partial(kernel, (nx, ny, T, D)), out_shape=tuple...]
    unnamed x17 -> x0, local copies, waits for them, and re-layouts: 8.89 us -> none
where the time goes in v2:
time: 83.7 us; the launch traced here: 83.6 us
  Pallas kernels  82.9 us (99%)
    pallas_call x1, Pallas kernels, step(): pl.pallas_call(functools.partial(kernel, (nx, ny, T, D)), out_shape=tuple...  81.5 us

profile of v2, /device:TPU:1, one launch (start us, length us, event | category | flops | bytes accessed | tf_op | source)
XLA Modules:
  0.0 83.6 jit_solution(15118545050665878635)
XLA Ops:
  0.6 81.5 %shard_map.101 = (bf16[1,2,1024]{2,1,0:T(2,128)(2,1)S(1)}, bf16[1,2,1024]{2,1,0:T(2,128)(2,1)S(1)}, bf16[1,512,1024]{2,1,0:T(8,128)(2,1)S(1)}, f32[1024,128]{1,0:T(8,128)S(1)}, f32[1024,128]{1,0:T(8,128)S(1)}) custom-call(bf16[1,512,1024]{2,1,0:T(8,128)(2,1)} %ctx_hbm.1, s32[1,4]{1,0:T(1,128)} %bv_ref.1, bf16[1024,128]{1,0:T(8,128)(2,1)} %kw_hbm.1, ...), custom_call_target="tpu_custom_call" | custom-call | tf_op jit(solution)/shard_map/pallas_call | solution.py:483
  82.2 1.4 %shard_map.102 = (bf16[1,2,1024]{2,1,0:T(2,128)(2,1)}, bf16[1,2,1024]{2,1,0:T(2,128)(2,1)}, bf16[1,512,1024]{2,1,0:T(8,128)(2,1)}, f32[1024,128]{1,0:T(8,128)}, f32[1024,128]{1,0:T(8,128)}) custom-call(bf16[1,2,1024]{2,1,0:T(2,128)(2,1)S(1)} %get-tuple-element.10.refs_0_, bf16[1,2,1024]{2,1,0:T(2,128)(2,1)S(1)} %get-tuple-element.11.refs_1_, ...), custom_call_target="tpu_custom_call" | custom-call | tf_op jit(solution)/shard_map/pallas_call | solution.py:518

commit v3 on v2

--- a/solution.py
+++ b/solution.py
@@ -44,7 +44,7 @@
     ctx, kw, vw, lq, og,
     blk, xblk, qg, dog, wg, kvx, kvr, ke, ko, ve, vo, bias,
     ctxo, ctxt, wsend, wrecv, sys_, syr, stz, sty, zsend, zrecv,
-    acc, dqs, dqr, dzs, dzr, dkv, dkvr, wsx, wrx, wps, wpr, wza, wxa, gx,
+    acc, accb, prob, psl, dqs, dqr, dzs, dzr, dkv, dkvr, wsx, wrx, wza, wxa, gx,
     a16, ax, d16, dx,
     s_in, s_core, r_core, s_ag, r_qz, r_y, r_rz, r_ry,
 ):
@@ -60,7 +60,8 @@
     oc = 1 - c
     base = pl.multiple_of((y * NZ + z) * 16, 16)
     yrows = pl.ds(pl.multiple_of(y * rows, rows), rows)
-    mexy = x * ny + y
+    ng = 2 * nxy
+    meg = lax.rem(z, 2) * nxy + x * ny + y
 
     def seq_of(zz, yy, cc):
         return (zz * ny + yy) * 2 + cc
@@ -76,9 +77,12 @@
         yt = lax.rem(y + j, ny)
         return yt, (seq_of(z, yt, c), x)
 
-    def xy_peer(j):
-        t = lax.rem(mexy + j, nxy)
-        return t, (seq_of(z, lax.rem(t, ny), c), t // ny)
+    def member(t):
+        r = lax.rem(t, nxy)
+        return (seq_of((z // 2) * 2 + t // nxy, lax.rem(r, ny), c), r // ny)
+
+    def group_peer(j):
+        return member(lax.rem(meg + j, ng))
 
     def spread(k, n):
         odd = lax.rem(k, 2)
@@ -108,9 +112,9 @@
         _, peer = z_peer(NZ // 2 + spread(k, NZ))
         pl.semaphore_signal(barrier, inc=1, device_id=peer, device_id_type=MESH)
 
-    @pl.loop(1, nxy)
+    @pl.loop(1, ng)
     def _(j):
-        pl.semaphore_signal(barrier, inc=1, device_id=xy_peer(j)[1], device_id_type=MESH)
+        pl.semaphore_signal(barrier, inc=1, device_id=group_peer(j), device_id_type=MESH)
 
     pl.semaphore_signal(barrier, inc=1, device_id=core_peer(), device_id_type=MESH)
 
@@ -164,7 +168,7 @@
         at = pl.ds(pl.multiple_of(i * 128, 128), 128)
         ctxt[:, at] = ctx[at, :].T
 
-    pl.semaphore_wait(barrier, 1 + (NZ - 1) + (nxy - 1))
+    pl.semaphore_wait(barrier, 1 + (NZ - 1) + (ng - 1))
 
     send(blk.at[oc], xblk, s_core.at[0], r_core.at[0], core_peer())
     send(kvx.at[oc], kvr, s_core.at[1], r_core.at[1], core_peer())
@@ -181,7 +185,6 @@
     oown = dog.at[pl.ds(base, 16), :]
     to_z(lambda zt, peer: send(qown, qown, s_ag.at[0], r_qz.at[z], peer))
     to_z(lambda zt, peer: send(oown, oown, s_ag.at[1], r_rz.at[0], peer))
-    send(ctx, ctxo, s_core.at[2], r_core.at[2], core_peer())
 
     wait(kvr, r_core.at[1])
     for part in range(2):
@@ -214,7 +217,7 @@
         part = dog.at[yrows, :]
         send(part, part, s_ag.at[3], r_y.at[1, y], y_peer(j)[1])
 
-    def forward(yb, wait_o, dst, sdst):
+    def forward(yb, wait_o, dst):
         outs, logs = [], []
         for h in range(rows // 128):
             r0 = pl.multiple_of(yb * rows + h * 128, 128)
@@ -240,20 +243,22 @@
             for k, val in ((0, logs[2 * h]), (1, logs[2 * h + 1]), (4, even), (5, odd)):
                 cols = jnp.where(lane == 2 * h + k, val, cols)
             stat = stat + cols.T[0:8, :]
-        sdst[yb] = stat
-
-    forward(y, lambda: None, wrecv, syr)
+        sys_[yb] = stat
+
+    forward(y, lambda: None, wrecv)
+    syr[y] = sys_[y]
 
     @pl.loop(1, ny)
     def _(j):
         yt, peer = y_peer(j)
         wait(qg.at[yrows, :], r_y.at[0, yt])
-        forward(yt, lambda: wait(dog.at[yrows, :], r_y.at[1, yt]), wsend, sys_)
+        forward(yt, lambda: wait(dog.at[yrows, :], r_y.at[1, yt]), wsend)
         send(sys_.at[yt], syr.at[y], s_ag.at[4], r_ry.at[0, y], peer)
 
     for j in range(1, ny):
         yt, peer = y_peer(j)
         send(wsend.at[yt], wrecv.at[y], s_ag.at[5], r_ry.at[1, y], peer)
+    send(ctx, ctxo, s_core.at[2], r_core.at[2], core_peer())
 
     for j in range(1, ny):
         yt, _ = y_peer(j)
@@ -261,6 +266,18 @@
     stz[z] = combine([syr[i] for i in range(ny)])
     to_z(lambda zt, peer: send(stz.at[z], stz.at[z], s_ag.at[6], r_rz.at[1], peer))
 
+    @pl.loop(0, ny)
+    def _(yb):
+        cols = jnp.concatenate([sys_[yb], jnp.zeros((120, 128), F32)], axis=0).T
+        for h in range(rows // 128):
+            at = pl.ds(pl.multiple_of(yb * rows + h * 128, 128), 128)
+            for eo, (kr, vr) in enumerate(((ke, ve), (ko, vo))):
+                k = 2 * h + eo
+                s = dot_nt(qg[at, :], kr[...]) + bias[...]
+                p = jnp.exp(s - cols[:, k:k + 1])
+                prob[eo, at, :] = p
+                psl[eo, at, :] = p * dot_nt(dog[at, :], vr[...])
+
     wait(ctxo, r_core.at[2])
 
     @pl.loop(0, T // 128)
@@ -276,23 +293,23 @@
         send(sty.at[y], sty.at[y], s_ag.at[7], r_ry.at[2, y], y_peer(j)[1])
 
     def backward(yb, dst):
-        cols = jnp.concatenate([sty[yb], jnp.zeros((120, 128), F32)], axis=0).T
+        full = sty[yb]
+        share = jnp.exp(jnp.minimum(sys_[yb] - full, 0.0))
+        tile = jnp.where(lax.broadcasted_iota(jnp.int32, (8, 128), 0) < 4, share, full)
+        cols = jnp.concatenate([tile, jnp.zeros((120, 128), F32)], axis=0).T
         grads = [[], []]
         probs = [[], []]
         qs, os = [], []
         for h in range(rows // 128):
-            r0 = pl.multiple_of(yb * rows + h * 128, 128)
-            q = qg[pl.ds(r0, 128), :]
-            o = dog[pl.ds(r0, 128), :]
-            qs.append(q)
-            os.append(o)
+            at = pl.ds(pl.multiple_of(yb * rows + h * 128, 128), 128)
+            qs.append(qg[at, :])
+            os.append(dog[at, :])
             out = jnp.zeros((128, 128), F32)
-            for eo, (kr, vr) in enumerate(((ke, ve), (ko, vo))):
+            for eo, kr in enumerate((ke, ko)):
                 k = 2 * h + eo
-                s = dot_nt(q, kr[...]) + bias[...]
-                p = jnp.exp(s - cols[:, k:k + 1])
-                slopes = dot_nt(o, vr[...])
-                ds = (p * (slopes - cols[:, 4 + k:5 + k])).astype(BF16)
+                f = cols[:, k:k + 1]
+                p = prob[eo, at, :] * f
+                ds = (psl[eo, at, :] * f - p * cols[:, 4 + k:5 + k]).astype(BF16)
                 probs[eo].append(p.astype(BF16))
                 grads[eo].append(ds)
                 out = out + dot_nn(ds, kr[...])
@@ -330,27 +347,33 @@
         backward(yt, dqs)
         send(dqs.at[yt], dqr.at[y], s_ag.at[9], r_ry.at[3, y], peer)
 
+    sl = D // ng
+    n = min(256, D)
+    per = n // sl
+    accb[...] = acc[...].astype(BF16)
+
+    @pl.loop(0, D // n)
+    def _(i):
+        at = lax.rem(meg // per + 1 + i, D // n)
+        g = dot_nt(ctxt[pl.ds(pl.multiple_of(at * n, n), n), :], accb[...])
+        wsx[pl.ds(at * per, per)] = g.reshape(per, sl, 128).astype(BF16)
+
+        @pl.loop(0, per)
+        def _(j):
+            t = at * per + j
+
+            @pl.when(t != meg)
+            def _():
+                send(wsx.at[t], wrx.at[meg], s_ag.at[10], r_rz.at[3], member(t))
+
+    wrx[meg] = wsx[meg]
+
     @pl.loop(0, TT // 128)
     def _(i):
         at = pl.ds(pl.multiple_of(i * 128, 128), 128)
         dkv[at, :] = acc[:, at].T.astype(BF16)
 
     send(dkv.at[pl.ds(T, T), :], dkvr, s_core.at[4], r_core.at[4], core_peer())
-
-    sl = D // nxy
-    n = min(256, D)
-
-    @pl.loop(0, D // n)
-    def _(i):
-        g = dot_nn(ctxt[pl.ds(pl.multiple_of(i * n, n), n), :], dkv[...])
-        wsx[pl.ds(i * (n // sl), n // sl)] = g.reshape(n // sl, sl, 128).astype(BF16)
-
-    @pl.loop(1, nxy)
-    def _(j):
-        t, peer = xy_peer(j)
-        send(wsx.at[t], wrx.at[mexy], s_ag.at[10], r_rz.at[3], peer)
-
-    wrx[mexy] = wsx[mexy]
 
     for j in range(1, ny):
         yt, _ = y_peer(j)
@@ -360,10 +383,13 @@
     to_z(lambda zt, peer: send(dzs.at[zt], dzr.at[z], s_ag.at[11], r_rz.at[4], peer))
     dzr[z] = dzs[z]
 
-    wait(wrx.at[pl.ds(0, nxy - 1)], r_rz.at[3])
-    wps[...] = jnp.sum(wrx[...].astype(F32), axis=0)
-    pair = (seq_of(z + 1 - 2 * lax.rem(z, 2), y, c), x)
-    send(wps, wpr, s_core.at[7], r_core.at[7], pair)
+    wait(wrx.at[pl.ds(0, ng - 1)], r_rz.at[3])
+    wza[z // 2] = jnp.sum(wrx[...].astype(F32), axis=0).astype(BF16)
+
+    @pl.loop(0, NZ // 2 - 1)
+    def _(k):
+        zt, peer = z_peer(NZ // 2 + 2 * spread(k, NZ // 2))
+        send(wza.at[z // 2], wza.at[z // 2], s_ag.at[12], r_rz.at[5], peer)
 
     wait(zrecv.at[pl.ds(0, NZ - 1)], r_rz.at[2])
     att = jnp.sum(zrecv[...].astype(F32), axis=0)
@@ -371,14 +397,6 @@
     a16[1] = att[8:]
     send(a16.at[oc], ax, s_core.at[3], r_core.at[3], core_peer())
 
-    wait(wpr, r_core.at[7])
-    wza[z // 2] = (wps[...] + wpr[...]).astype(BF16)
-
-    @pl.loop(0, NZ // 2 - 1)
-    def _(k):
-        zt, peer = z_peer(NZ // 2 + 2 * spread(k, NZ // 2))
-        send(wza.at[z // 2], wza.at[z // 2], s_ag.at[12], r_rz.at[5], peer)
-
     wait(dkvr, r_core.at[4])
 
     @pl.loop(0, T // 128)
@@ -394,12 +412,11 @@
     send(d16.at[oc], dx, s_core.at[5], r_core.at[5], core_peer())
 
     wait(wza.at[pl.ds(0, NZ // 2 - 1)], r_rz.at[5])
-    wxa[mexy] = jnp.sum(wza[...].astype(F32), axis=0).astype(BF16)
-
-    @pl.loop(1, nxy)
+    wxa[meg] = jnp.sum(wza[...].astype(F32), axis=0).astype(BF16)
+
+    @pl.loop(1, ng)
     def _(j):
-        t, peer = xy_peer(j)
-        send(wxa.at[mexy], wxa.at[mexy], s_ag.at[13], r_rz.at[6], peer)
+        send(wxa.at[meg], wxa.at[meg], s_ag.at[13], r_rz.at[6], group_peer(j))
 
     def own_rows(mine8, other8):
         f8 = jnp.where(c == 0, mine8, other8)
@@ -421,7 +438,6 @@
     wait(ax, s_core.at[3])
     wait(dkvr, s_core.at[4])
     wait(dx, s_core.at[5])
-    wait(wpr, s_core.at[7])
     for i in range(2):
         wait(qg.at[pl.ds(0, (NZ - 1) * 16), :], s_ag.at[i])
         wait(qg.at[pl.ds(0, (ny - 1) * rows), :], s_ag.at[2 + i])
@@ -431,13 +447,13 @@
     wait(sty.at[pl.ds(0, ny - 1)], s_ag.at[7])
     wait(zrecv.at[pl.ds(0, NZ - 1)], s_ag.at[8])
     wait(dqr.at[pl.ds(0, ny - 1)], s_ag.at[9])
-    wait(wrx.at[pl.ds(0, nxy - 1)], s_ag.at[10])
+    wait(wrx.at[pl.ds(0, ng - 1)], s_ag.at[10])
     wait(dzr.at[pl.ds(0, NZ - 1)], s_ag.at[11])
     wait(wza.at[pl.ds(0, NZ // 2 - 1)], s_ag.at[12])
 
-    wait(wxa.at[pl.ds(0, nxy - 1)], r_rz.at[6])
+    wait(wxa.at[pl.ds(0, ng - 1)], r_rz.at[6])
     send(wxa, gx, s_core.at[6], r_core.at[6], core_peer())
-    wait(wxa.at[pl.ds(0, nxy - 1)], s_ag.at[13])
+    wait(wxa.at[pl.ds(0, ng - 1)], s_ag.at[13])
     wait(gx, r_core.at[6])
     ga = wxa[...].astype(F32).reshape(D, 128)
     gb = gx[...].astype(F32).reshape(D, 128)
@@ -466,8 +482,8 @@
         T, D = context.shape[1:]
         rows = NZ * 16
         nr = ny * rows
-        nxy = nx * ny
-        sl = D // nxy
+        ng = 2 * nx * ny
+        sl = D // ng
         vm = lambda shape, dtype=F32: pltpu.VMEM(shape, dtype)
         vmem = pl.BlockSpec(memory_space=pltpu.VMEM)
         smem = pl.BlockSpec(memory_space=pltpu.SMEM)
@@ -499,16 +515,16 @@
                 vm((ny, rows, 128), BF16), vm((ny, rows, 128), BF16),
                 vm((ny, 8, 128)), vm((ny, 8, 128)), vm((NZ, 8, 128)), vm((ny, 8, 128)),
                 vm((NZ, 16, 128), BF16), vm((NZ, 16, 128), BF16),
-                vm((128, 2 * T)),
+                vm((128, 2 * T)), vm((128, 2 * T), BF16),
+                vm((2, nr, 2 * T)), vm((2, nr, 2 * T)),
                 vm((ny, rows, 128), BF16), vm((ny, rows, 128), BF16),
                 vm((NZ, 16, 128), BF16), vm((NZ, 16, 128), BF16),
                 vm((2 * T, 128), BF16), vm((T, 128), BF16),
-                vm((nxy, sl, 128), BF16), vm((nxy, sl, 128), BF16),
-                vm((sl, 128)), vm((sl, 128)),
+                vm((ng, sl, 128), BF16), vm((ng, sl, 128), BF16),
                 vm((NZ // 2, sl, 128), BF16),
-                vm((nxy, sl, 128), BF16), vm((nxy, sl, 128), BF16),
+                vm((ng, sl, 128), BF16), vm((ng, sl, 128), BF16),
                 vm((2, 8, 128)), vm((8, 128)), vm((2, 8, 128)), vm((8, 128)),
-                dma((5,)), dma((8,)), dma((8,)), dma((14,)), dma((NZ,)), dma((2, ny)),
+                dma((5,)), dma((7,)), dma((7,)), dma((14,)), dma((NZ,)), dma((2, ny)),
                 dma((7,)), dma((4, ny)),
             ],
             compiler_params=pltpu.CompilerParams(

time: 83.7 us -> 79.2 us (0.946)
  Pallas kernels: 82.9 us -> 78.4 us
    pallas_call x1, Pallas kernels: 81.5 us -> 77.1 us  [step(): pl.pallas_call(functools.partial(kernel, (nx, ny, T, D)), out_shape=tuple...]
where the time goes in v3:
time: 79.2 us; the launch traced here: 79.1 us
  Pallas kernels  78.4 us (99%)
    pallas_call x1, Pallas kernels, step(): pl.pallas_call(functools.partial(kernel, (nx, ny, T, D)), out_shape=tuple...  77.1 us

profile of v3, /device:TPU:1, one launch (start us, length us, event | category | flops | bytes accessed | tf_op | source)
XLA Modules:
  0.0 79.1 jit_solution(15579174694892238570)
XLA Ops:
  0.6 77.1 %shard_map.101 = (bf16[1,2,1024]{2,1,0:T(2,128)(2,1)S(1)}, bf16[1,2,1024]{2,1,0:T(2,128)(2,1)S(1)}, bf16[1,512,1024]{2,1,0:T(8,128)(2,1)S(1)}, f32[1024,128]{1,0:T(8,128)S(1)}, f32[1024,128]{1,0:T(8,128)S(1)}) custom-call(bf16[1,512,1024]{2,1,0:T(8,128)(2,1)} %ctx_hbm.1, s32[1,4]{1,0:T(1,128)} %bv_ref.1, bf16[1024,128]{1,0:T(8,128)(2,1)} %kw_hbm.1, ...), custom_call_target="tpu_custom_call" | custom-call | tf_op jit(solution)/shard_map/pallas_call | solution.py:499
  77.7 1.4 %shard_map.102 = (bf16[1,2,1024]{2,1,0:T(2,128)(2,1)}, bf16[1,2,1024]{2,1,0:T(2,128)(2,1)}, bf16[1,512,1024]{2,1,0:T(8,128)(2,1)}, f32[1024,128]{1,0:T(8,128)}, f32[1024,128]{1,0:T(8,128)}) custom-call(bf16[1,2,1024]{2,1,0:T(2,128)(2,1)S(1)} %get-tuple-element.10.refs_0_, bf16[1,2,1024]{2,1,0:T(2,128)(2,1)S(1)} %get-tuple-element.11.refs_1_, ...), custom_call_target="tpu_custom_call" | custom-call | tf_op jit(solution)/shard_map/pallas_call | solution.py:534

commit v4 on v3

--- a/solution.py
+++ b/solution.py
@@ -46,7 +46,7 @@
     ctxo, ctxt, wsend, wrecv, sys_, syr, stz, sty, zsend, zrecv,
     acc, accb, prob, psl, dqs, dqr, dzs, dzr, dkv, dkvr, wsx, wrx, wza, wxa, gx,
     a16, ax, d16, dx,
-    s_in, s_core, r_core, s_ag, r_qz, r_y, r_rz, r_ry,
+    s_in, s_core, r_core, s_ag, r_qz, r_oz, r_y, r_rz, r_ry,
 ):
     nx, ny, T, D = dims
     rows = NZ * 16
@@ -140,6 +140,23 @@
                     pieces.append(src[l:l + 1, at:at + 128])
         blk[g] = jnp.concatenate(pieces, axis=0).astype(BF16)
 
+    pl.semaphore_wait(barrier, 1 + (NZ - 1) + (ng - 1))
+
+    send(blk.at[oc], xblk, s_core.at[0], r_core.at[0], core_peer())
+
+    wait(xblk, r_core.at[0])
+    own = blk[c].astype(F32)
+    oth = xblk[...].astype(F32)
+    first = jnp.where(c == 0, own, oth)
+    second = jnp.where(c == 0, oth, own)
+    qg[pl.ds(base, 16), :] = jnp.concatenate([first[:8], second[:8]], axis=0).astype(BF16)
+    dog[pl.ds(base, 16), :] = jnp.concatenate([first[8:], second[8:]], axis=0).astype(BF16)
+
+    qown = qg.at[pl.ds(base, 16), :]
+    oown = dog.at[pl.ds(base, 16), :]
+    to_z(lambda zt, peer: send(qown, qown, s_ag.at[0], r_qz.at[z], peer))
+    to_z(lambda zt, peer: send(oown, oown, s_ag.at[1], r_oz.at[z], peer))
+
     loads[2].wait()
     loads[3].wait()
     kwf = kw[...].astype(F32)
@@ -163,28 +180,12 @@
     kvx[0, T:T + 16, :] = flags.astype(BF16)
     kvx[1, T:T + 16, :] = flags.astype(BF16)
 
+    send(kvx.at[oc], kvr, s_core.at[1], r_core.at[1], core_peer())
+
     @pl.loop(0, T // 128)
     def _(i):
         at = pl.ds(pl.multiple_of(i * 128, 128), 128)
         ctxt[:, at] = ctx[at, :].T
-
-    pl.semaphore_wait(barrier, 1 + (NZ - 1) + (ng - 1))
-
-    send(blk.at[oc], xblk, s_core.at[0], r_core.at[0], core_peer())
-    send(kvx.at[oc], kvr, s_core.at[1], r_core.at[1], core_peer())
-
-    wait(xblk, r_core.at[0])
-    own = blk[c].astype(F32)
-    oth = xblk[...].astype(F32)
-    first = jnp.where(c == 0, own, oth)
-    second = jnp.where(c == 0, oth, own)
-    qg[pl.ds(base, 16), :] = jnp.concatenate([first[:8], second[:8]], axis=0).astype(BF16)
-    dog[pl.ds(base, 16), :] = jnp.concatenate([first[8:], second[8:]], axis=0).astype(BF16)
-
-    qown = qg.at[pl.ds(base, 16), :]
-    oown = dog.at[pl.ds(base, 16), :]
-    to_z(lambda zt, peer: send(qown, qown, s_ag.at[0], r_qz.at[z], peer))
-    to_z(lambda zt, peer: send(oown, oown, s_ag.at[1], r_rz.at[0], peer))
 
     wait(kvr, r_core.at[1])
     for part in range(2):
@@ -200,38 +201,34 @@
         for j in range(T // BLK):
             bias[:, part * T + j * BLK:part * T + (j + 1) * BLK] = fl[j:j + 1, :]
 
-    @pl.loop(0, NZ)
-    def _(k):
-        zs = lax.rem(z + spread(k, NZ), NZ)
-        part = qg.at[pl.ds(pl.multiple_of((y * NZ + zs) * 16, 16), 16), :]
-
-        @pl.when(k > 0)
-        def _():
-            wait(part, r_qz.at[zs])
-
-        for j in range(1, ny):
-            send(part, part, s_ag.at[2], r_y.at[0, y], y_peer(j)[1])
-
-    wait(dog.at[pl.ds(0, (NZ - 1) * 16), :], r_rz.at[0])
-    for j in range(1, ny):
-        part = dog.at[yrows, :]
-        send(part, part, s_ag.at[3], r_y.at[1, y], y_peer(j)[1])
-
-    def forward(yb, wait_o, dst):
+    def pass_on(n, buf, sems):
+        @pl.loop(0, NZ)
+        def _(k):
+            zs = lax.rem(z + spread(k, NZ), NZ)
+            part = buf.at[pl.ds(pl.multiple_of((y * NZ + zs) * 16, 16), 16), :]
+
+            @pl.when(k > 0)
+            def _():
+                wait(part, sems.at[zs])
+
+            for j in range(1, ny):
+                send(part, part, s_ag.at[2 + n], r_y.at[n, y], y_peer(j)[1])
+
+    pass_on(0, qg, r_qz)
+
+    def forward(yb, wait_o):
         outs, logs = [], []
-        for h in range(rows // 128):
-            r0 = pl.multiple_of(yb * rows + h * 128, 128)
-            q = qg[pl.ds(r0, 128), :]
-            out = jnp.zeros((128, 128), F32)
-            for kr, vr in ((ke, ve), (ko, vo)):
-                s = dot_nt(q, kr[...]) + bias[...]
-                m = jnp.max(s, axis=1, keepdims=True)
-                p = jnp.exp(s - m)
-                l = jnp.sum(p, axis=1, keepdims=True)
-                out = out + dot_nn(p.astype(BF16), vr[...]) / l
-                logs.append(m + jnp.log(l))
-            dst[yb, h * 128:(h + 1) * 128, :] = out.astype(BF16)
+        hs = range(rows // 128)
+        at = [pl.ds(pl.multiple_of(yb * rows + h * 128, 128), 128) for h in hs]
+        s = [[dot_nt(qg[at[h], :], kr[...]) + bias[...] for kr in (ke, ko)] for h in hs]
+        m = [[jnp.max(v, axis=1, keepdims=True) for v in pair] for pair in s]
+        p = [[jnp.exp(v - w) for v, w in zip(*pair)] for pair in zip(s, m)]
+        l = [[jnp.sum(v, axis=1, keepdims=True) for v in pair] for pair in p]
+        for h in hs:
+            out = dot_nn(p[h][0].astype(BF16), ve[...]) / l[h][0] + dot_nn(p[h][1].astype(BF16), vo[...]) / l[h][1]
+            wsend[yb, h * 128:(h + 1) * 128, :] = out.astype(BF16)
             outs.append(out)
+            logs += [m[h][i] + jnp.log(l[h][i]) for i in range(2)]
         wait_o()
         stat = jnp.zeros((8, 128), F32)
         for h in range(rows // 128):
@@ -245,16 +242,31 @@
             stat = stat + cols.T[0:8, :]
         sys_[yb] = stat
 
-    forward(y, lambda: None, wrecv)
-    syr[y] = sys_[y]
-
-    @pl.loop(1, ny)
+    @pl.loop(0, ny)
     def _(j):
         yt, peer = y_peer(j)
-        wait(qg.at[yrows, :], r_y.at[0, yt])
-        forward(yt, lambda: wait(dog.at[yrows, :], r_y.at[1, yt]), wsend)
-        send(sys_.at[yt], syr.at[y], s_ag.at[4], r_ry.at[0, y], peer)
-
+
+        @pl.when(j > 0)
+        def _():
+            wait(qg.at[yrows, :], r_y.at[0, yt])
+
+        def cotangents():
+            @pl.when(j == 0)
+            def _():
+                pass_on(1, dog, r_oz)
+
+            @pl.when(j > 0)
+            def _():
+                wait(dog.at[yrows, :], r_y.at[1, yt])
+
+        forward(yt, cotangents)
+
+        @pl.when(j > 0)
+        def _():
+            send(sys_.at[yt], syr.at[y], s_ag.at[4], r_ry.at[0, y], peer)
+
+    syr[y] = sys_[y]
+    wrecv[y] = wsend[y]
     for j in range(1, ny):
         yt, peer = y_peer(j)
         send(wsend.at[yt], wrecv.at[y], s_ag.at[5], r_ry.at[1, y], peer)
@@ -292,7 +304,7 @@
     for j in range(1, ny):
         send(sty.at[y], sty.at[y], s_ag.at[7], r_ry.at[2, y], y_peer(j)[1])
 
-    def backward(yb, dst):
+    def backward(yb):
         full = sty[yb]
         share = jnp.exp(jnp.minimum(sys_[yb] - full, 0.0))
         tile = jnp.where(lax.broadcasted_iota(jnp.int32, (8, 128), 0) < 4, share, full)
@@ -313,39 +325,49 @@
                 probs[eo].append(p.astype(BF16))
                 grads[eo].append(ds)
                 out = out + dot_nn(ds, kr[...])
-            dst[yb, h * 128:(h + 1) * 128, :] = (out * (HD ** -0.5)).astype(BF16)
+            dqs[yb, h * 128:(h + 1) * 128, :] = (out * (HD ** -0.5)).astype(BF16)
         cat = lambda parts: jnp.concatenate(parts, axis=0)
         qt = cat(qs).T
         ot = cat(os).T
         acc[0:64, :] += dot_nn(qt[:64], cat(grads[0])) + dot_nn(qt[64:], cat(grads[1]))
         acc[64:128, :] += dot_nn(ot[:64], cat(probs[0])) + dot_nn(ot[64:], cat(probs[1]))
 
-    backward(y, dqr)
-
-    for j in range(1, ny):
-        yt, _ = y_peer(j)
-        wait(wrecv.at[yt], r_ry.at[1, yt])
-    full = sty[y]
-    coef = jnp.concatenate(
-        [jnp.exp(jnp.minimum(syr[i] - full, 0.0)) for i in range(ny)]
-        + [jnp.zeros((128 - 8 * ny, 128), F32)], axis=0
-    ).T
-    for h in range(rows // 128):
-        w = jnp.zeros((128, 128), F32)
-        for i in range(ny):
-            k = i * 8 + 2 * h
-            w = w + wrecv[i, h * 128:(h + 1) * 128, :].astype(F32) * jnp.where(
-                lo, coef[:, k:k + 1], coef[:, k + 1:k + 2])
-        zsend[8 * h:8 * h + 8] = w.reshape(8, 16, 128).astype(BF16)
-    to_z(lambda zt, peer: send(zsend.at[zt], zrecv.at[z], s_ag.at[8], r_rz.at[2], peer))
-    zrecv[z] = zsend[z]
-
-    @pl.loop(1, ny)
+    def weighted():
+        for j in range(1, ny):
+            yt, _ = y_peer(j)
+            wait(wrecv.at[yt], r_ry.at[1, yt])
+        full = sty[y]
+        coef = jnp.concatenate(
+            [jnp.exp(jnp.minimum(syr[i] - full, 0.0)) for i in range(ny)]
+            + [jnp.zeros((128 - 8 * ny, 128), F32)], axis=0
+        ).T
+        for h in range(rows // 128):
+            w = jnp.zeros((128, 128), F32)
+            for i in range(ny):
+                k = i * 8 + 2 * h
+                w = w + wrecv[i, h * 128:(h + 1) * 128, :].astype(F32) * jnp.where(
+                    lo, coef[:, k:k + 1], coef[:, k + 1:k + 2])
+            zsend[8 * h:8 * h + 8] = w.reshape(8, 16, 128).astype(BF16)
+        to_z(lambda zt, peer: send(zsend.at[zt], zrecv.at[z], s_ag.at[8], r_rz.at[2], peer))
+        zrecv[z] = zsend[z]
+
+    @pl.loop(0, ny)
     def _(j):
         yt, peer = y_peer(j)
-        wait(sty.at[y], r_ry.at[2, yt])
-        backward(yt, dqs)
-        send(dqs.at[yt], dqr.at[y], s_ag.at[9], r_ry.at[3, y], peer)
+
+        @pl.when(j > 0)
+        def _():
+            wait(sty.at[y], r_ry.at[2, yt])
+
+        backward(yt)
+
+        @pl.when(j == 0)
+        def _():
+            weighted()
+
+        @pl.when(j > 0)
+        def _():
+            send(dqs.at[yt], dqr.at[y], s_ag.at[9], r_ry.at[3, y], peer)
 
     sl = D // ng
     n = min(256, D)
@@ -375,6 +397,7 @@
 
     send(dkv.at[pl.ds(T, T), :], dkvr, s_core.at[4], r_core.at[4], core_peer())
 
+    dqr[y] = dqs[y]
     for j in range(1, ny):
         yt, _ = y_peer(j)
         wait(dqr.at[yt], r_ry.at[3, yt])
@@ -524,7 +547,7 @@
                 vm((NZ // 2, sl, 128), BF16),
                 vm((ng, sl, 128), BF16), vm((ng, sl, 128), BF16),
                 vm((2, 8, 128)), vm((8, 128)), vm((2, 8, 128)), vm((8, 128)),
-                dma((5,)), dma((7,)), dma((7,)), dma((14,)), dma((NZ,)), dma((2, ny)),
+                dma((5,)), dma((7,)), dma((7,)), dma((14,)), dma((NZ,)), dma((NZ,)), dma((2, ny)),
                 dma((7,)), dma((4, ny)),
             ],
             compiler_params=pltpu.CompilerParams(

time: 79.2 us -> 76.1 us (0.961)
  Pallas kernels: 78.4 us -> 75.3 us
    pallas_call x1, Pallas kernels: 77.1 us -> 73.9 us  [step(): pl.pallas_call(functools.partial(kernel, (nx, ny, T, D)), out_shape=tuple...]
where the time goes in v4:
time: 76.1 us; the launch traced here: 75.9 us
  Pallas kernels  75.3 us (99%)
    pallas_call x1, Pallas kernels, step(): pl.pallas_call(functools.partial(kernel, (nx, ny, T, D)), out_shape=tuple...  73.9 us

profile of v4, /device:TPU:1, one launch (start us, length us, event | category | flops | bytes accessed | tf_op | source)
XLA Modules:
  0.0 75.9 jit_solution(15677646023698152290)
XLA Ops:
  0.6 73.9 %shard_map.101 = (bf16[1,2,1024]{2,1,0:T(2,128)(2,1)S(1)}, bf16[1,2,1024]{2,1,0:T(2,128)(2,1)S(1)}, bf16[1,512,1024]{2,1,0:T(8,128)(2,1)S(1)}, f32[1024,128]{1,0:T(8,128)S(1)}, f32[1024,128]{1,0:T(8,128)S(1)}) custom-call(bf16[1,512,1024]{2,1,0:T(8,128)(2,1)} %ctx_hbm.1, s32[1,4]{1,0:T(1,128)} %bv_ref.1, bf16[1024,128]{1,0:T(8,128)(2,1)} %kw_hbm.1, ...), custom_call_target="tpu_custom_call" | custom-call | tf_op jit(solution)/shard_map/pallas_call | solution.py:522
  74.6 1.4 %shard_map.102 = (bf16[1,2,1024]{2,1,0:T(2,128)(2,1)}, bf16[1,2,1024]{2,1,0:T(2,128)(2,1)}, bf16[1,512,1024]{2,1,0:T(8,128)(2,1)}, f32[1024,128]{1,0:T(8,128)}, f32[1024,128]{1,0:T(8,128)}) custom-call(bf16[1,2,1024]{2,1,0:T(2,128)(2,1)S(1)} %get-tuple-element.10.refs_0_, bf16[1,2,1024]{2,1,0:T(2,128)(2,1)S(1)} %get-tuple-element.11.refs_1_, ...), custom_call_target="tpu_custom_call" | custom-call | tf_op jit(solution)/shard_map/pallas_call | solution.py:557
